TPU v7x, 1024 devices: a whole 4x4x32 slice. The times are simulated.
1024 devices in a mesh: dp: 32 (over z), expert: 8 (over x, core), tensor: 4 (over y).
Axes of the slice: x: 4, y: 4, z: 32, core: 2. Of those that a mesh axis runs over, the one named last changes fastest.
Arguments:
- out_grad: bfloat16 [4096, 6144], P('expert', 'dp'), may hold values from -0.796875 to 0.796875
- expert_ids: int32 [4096, 2], P('expert'), may hold values from 0 to 7, all different within a row; in each aligned block of 512 rows (0 to 511, 512 to 1023, ...) at most 192 rows name the same one
- combine: float32 [4096, 2], P('expert'), may hold values from 0.2 to 1
- hidden: bfloat16 [8, 1536, 16384], P('expert', 'dp', 'tensor'), may hold values from -6 to 6
Outputs:
- grad_down: bfloat16 [8, 16384, 6144], P('expert', 'tensor', 'dp')
Inputs may be any that keep to these rules, and one draw needn't show every extreme that they name: `expert_ids`: each row names 2 different experts; among the 512 rows of one device no expert is named more than 192 times.
All inputs are finite; a program needn't handle non-finite values.
Results may differ from a plain program's by a relative error of at most 0.0049.
Values may be sent and summed in bfloat16 or wider, within the bound.
No kernel may reach another device: no remote copies, remote signals or barrier semaphores. Data moves between devices by JAX's collectives and lax.ppermute only.
A program may use at most 64 MiB of HBM per device.

v0:
```python
import jax
import jax.numpy as jnp
from jax import lax
from jax.sharding import PartitionSpec as P

TOP = 2


def prefix(array, axis, combine, identity):
    size, place = (lax.axis_size(axis), lax.axis_index(axis))
    everything = lax.all_gather(array, axis)
    start = jnp.broadcast_to(jnp.asarray(identity, array.dtype), array.shape)

    def hop(k, before):
        reached = k < place
        new = combine(before, everything[k])
        return jnp.where(reached, new, before)

    return lax.fori_loop(0, size, hop, start)


def add_counts(earlier, later):
    return earlier + later


def body(out_grad, expert_ids, combine, hidden):
    experts = lax.axis_size("expert")
    features = out_grad.shape[1]
    capacity = hidden.shape[1] * lax.axis_size("dp")
    block_most = 3 * out_grad.shape[0] * TOP // (2 * experts)
    expert_range = jnp.arange(experts, dtype=jnp.int32)
    gradient, routed, weights = (out_grad, expert_ids, combine)
    onehot = (routed.reshape(-1)[:, None] == expert_range[None, :]).astype(jnp.int32)
    counts = jnp.sum(onehot, axis=0)
    offsets = prefix(counts, "expert", add_counts, jnp.zeros_like(counts))
    local_rank = jnp.sum((jnp.cumsum(onehot, axis=0) - onehot) * onehot, axis=1)
    slot_number = jnp.sum(onehot * offsets[None, :], axis=1) + local_rank
    scaled = (
        (weights[:, :, None] * gradient[:, None, :].astype(jnp.float32))
        .astype(jnp.bfloat16)
        .reshape(-1, features)
    )
    send_index = routed.reshape(-1) * block_most + local_rank
    send_rows = jnp.zeros((experts * block_most, features), jnp.bfloat16).at[send_index].set(scaled)
    send_slots = (
        jnp.full((experts * block_most,), capacity, jnp.int32).at[send_index].set(slot_number)
    )
    send_rows = send_rows.reshape(experts, block_most, features)
    send_slots = send_slots.reshape(experts, block_most)
    arrived_rows, arrived_slots = (
        lax.all_to_all(send_rows, "expert", split_axis=0, concat_axis=0, tiled=True),
        lax.all_to_all(send_slots, "expert", split_axis=0, concat_axis=0, tiled=True),
    )
    arranged = jnp.zeros((capacity + 1, features), jnp.bfloat16)
    arranged = arranged.at[arrived_slots.reshape(-1)].set(arrived_rows.reshape(-1, features))[
        :capacity
    ]
    gradient_sum = lax.dot_general(
        lax.all_gather(hidden[0], "dp", axis=0, tiled=True),
        arranged,
        (((0,), (0,)), ((), ())),
        preferred_element_type=jnp.float32,
    )
    return gradient_sum.astype(jnp.bfloat16)[None]


def solution(mesh):
    return jax.shard_map(
        body,
        mesh=mesh,
        in_specs=(
            P("expert", "dp"),
            P("expert", None),
            P("expert", None),
            P("expert", "dp", "tensor"),
        ),
        out_specs=P("expert", "tensor", "dp"),
        check_vma=False,
    )
```

profile of v0, /device:TPU:24, one launch (start us, length us, event | category | flops | bytes accessed | tf_op | source)
XLA Modules:
  0.0 201.2 jit_solution(575458281805874580)
XLA Ops:
  6.5 0.0 all-gather.4.cloned.1.call-start
  6.5 0.7 all-gather.4.cloned.1.call-update
  7.3 0.8 copy.7
  8.1 0.2 eq.25
  8.3 0.2 eq.29
  8.5 0.7 broadcast_multiply_fusion
  9.1 0.1 copy.6
  9.3 0.2 mul.47
  9.5 1.3 dynamic-slice
  11.5 0.1 convert_reduce_fusion
  11.6 0.2 dynamic-update-slice
  11.9 9.2 %all-reduce = s32[64]{0:T(128)S(1)} all-reduce(s32[64]{0:T(128)S(1)} %dynamic-update-slice), channel_id=2, replica_groups=mesh['dp'=32,'expert'=8,'tensor'=4] {'expert'}, use_global_device_ids=true, to_apply=%add | all-reduce | flops 64 | bytes 512
  21.1 0.1 reshape.124
  21.2 2.3 %reduce-window.6 = s32[8,8,128]{2,1,0:T(8,128)S(1)} reduce-window(s32[8,8,128]{2,1,0:T(8,128)S(1)} %fusion.16, s32[]{:T(128)} %constant.44.clone.1), window={size=1x1x128 pad=0_0x0_0x127_0}, to_apply=%region_0.0 | reduce-window | flops 1040384 | bytes 65540 | tf_op jit(solution)/shard_map/reduce-window
  23.5 0.3 slice_reduce_fusion
  23.7 0.2 reduce-window.9
  23.9 0.1 add_bitcast_fusion
  24.0 0.3 while.14
  24.3 0.1 select_reduce_fusion
  24.4 4.3 %scatter_custom_fusion = s32[1536]{0:T(1024)S(1)} fusion(s32[1024]{0:T(1024)S(1)} %bitcast.37, s32[1024]{0:T(1024)S(1)} %add.67, s32[]{:T(128)} %constant.42.clone.1), kind=kCustom, calls=%fused_computation.30 | custom fusion | bytes 6148 | tf_op jit(solution)/shard_map/scatter | solution.py:46
  28.7 0.7 all_to_all.9
  29.4 3.3 %all-to-all-start = ((s32[8,1,192]{2,1,0:T(1,128)}), s32[8,1,192]{2,1,0:T(1,128)S(1)}, u32[]{:S(2)}, u32[]{:S(2)}) async-start(s32[8,1,192]{2,1,0:T(1,128)} %all_to_all.9), calls=%async_computation | async-start | bytes 16384 | tf_op jit(solution)/shard_map/all_to_all | solution.py:52
  32.7 0.8 copy.9
  33.6 0.2 mul.51
  33.7 1.1 copy.10
  34.8 0.4 mul.53
  35.2 0.7 mul.54
  35.9 6.3 %scatter_custom_fusion.1 = bf16[1536,192]{1,0:T(8,128)(2,1)} fusion(s32[1024]{0:T(1024)S(1)} %bitcast.38, f32[1024,192]{1,0:T(8,128)S(1)} %mul.54, f32[1024]{0:T(1024)S(1)} %mul.51, bf16[]{:T(256)} %constant.41.clone.1), kind=kCustom, calls=%fused_computation.11 | custom fusion | flops 393216 | bytes 1642498 | tf_op jit(solution)/shard_map/scatter | solution.py:44
  42.2 0.0 all-to-all-done
  42.2 4.7 %all-to-all-start.1 = ((bf16[8,192,192]{2,1,0:T(8,128)(2,1)}), bf16[8,192,192]{2,1,0:T(8,128)(2,1)S(1)}, u32[]{:S(2)}, u32[]{:S(2)}) async-start(bf16[8,192,192]{2,1,0:T(8,128)(2,1)} %bitcast.4), calls=%async_computation.1 | async-start | bytes 1572864 | tf_op jit(solution)/shard_map/all_to_all | solution.py:51
  47.0 0.1 reshape.97
  47.1 13.0 %all-to-all-done.1 = bf16[8,192,192]{2,1,0:T(8,128)(2,1)S(1)} async-done(((bf16[8,192,192]{2,1,0:T(8,128)(2,1)}), bf16[8,192,192]{2,1,0:T(8,128)(2,1)S(1)}, u32[]{:S(2)}, u32[]{:S(2)}) %all-to-all-start.1) | async-done | bytes 589856 | tf_op jit(solution)/shard_map/all_to_all | solution.py:51
  60.1 7.5 %scatter_custom_fusion.2 = bf16[1537,192]{1,0:T(8,128)(2,1)S(1)} fusion(s32[1536]{0:T(1024)S(1)} %fusion.17, bf16[1536,192]{1,0:T(8,128)(2,1)S(1)} %bitcast.34, bf16[]{:T(256)} %constant.41.clone.1), kind=kCustom, calls=%fused_computation.13 | custom fusion | bytes 590210 | tf_op jit(solution)/shard_map/scatter | solution.py:55
  67.6 118.4 %all-gather.4.cloned.1.call-done = bf16[1,1536,4096]{2,1,0:T(8,128)(2,1)} async-done(((bf16[1,48,4096]{2,1,0:T(8,128)(2,1)}), bf16[1,1536,4096]{2,1,0:T(8,128)(2,1)}) %all-gather.4.cloned.1.call-update) | async-done | bytes 12582928 | tf_op jit(solution)/shard_map/all_gather | solution.py:59
  185.9 8.4 %fusion.5 = bf16[1,4096,192]{1,2,0:T(8,128)(2,1)} fusion(bf16[1,1536,4096]{2,1,0:T(8,128)(2,1)} %all-gather.4.cloned.1.call-done, bf16[1537,192]{1,0:T(8,128)(2,1)S(1)} %scatter_custom_fusion.2), kind=kOutput, calls=%fused_computation.8 | convolution fusion | flops 2416705536 | bytes 14942208 | tf_op jit(solution)/shard_map/dot_general | solution.py:58
  (15 shorter events, 0.2 us)
Async XLA Ops:
  6.5 179.4 %all-gather.4.cloned.1.call-start = ((), (), s32[]{:S(2)}) async-start(), calls=%async_computation.2 | async-start | bytes 12976128 | tf_op jit(solution)/shard_map/all_gather | solution.py:59
  29.4 12.8 %all-to-all-start = ((s32[8,1,192]{2,1,0:T(1,128)}), s32[8,1,192]{2,1,0:T(1,128)S(1)}, u32[]{:S(2)}, u32[]{:S(2)}) async-start(s32[8,1,192]{2,1,0:T(1,128)} %all_to_all.9), calls=%async_computation | async-start | bytes 16384 | tf_op jit(solution)/shard_map/all_to_all | solution.py:52
  42.2 17.9 %all-to-all-start.1 = ((bf16[8,192,192]{2,1,0:T(8,128)(2,1)}), bf16[8,192,192]{2,1,0:T(8,128)(2,1)S(1)}, u32[]{:S(2)}, u32[]{:S(2)}) async-start(bf16[8,192,192]{2,1,0:T(8,128)(2,1)} %bitcast.4), calls=%async_computation.1 | async-start | bytes 1572864 | tf_op jit(solution)/shard_map/all_to_all | solution.py:51
Sparse Core Ops, SparseCore 0:
  10.0 175.8 all-gather.3
where the time goes:
time: 202 us; the launch traced here: 201 us
  waiting for transfers between devices  132 us (65%)
  local copies, waits for them, and re-layouts  19.1 us (9%)
  between operations  14.2 us (7%)
  other arithmetic  9.93 us (5%)
  blocking collectives  9.22 us (5%)
  matrix products  8.38 us (4%)
  starting transfers between devices  8.04 us (4%)
    all_gather x1, waiting for transfers between devices, body(): lax.all_gather(hidden[0], 'dp', axis=0, tiled=True)  118 us
    all_to_all x1, waiting for transfers between devices, body(): lax.all_to_all(send_rows, 'expert', split_axis=0, concat_axis=0, tiled=True)  13 us
    unnamed x1, blocking collectives  9.22 us
    dot_general x1, matrix products, body(): lax.dot_general(lax.all_gather(hidden[0], 'dp', axis=0, tiled=True), arra...  8.38 us
    scatter x1, local copies, waits for them, and re-layouts, body(): arranged.at[arrived_slots.reshape(-1)]  7.47 us
    scatter x1, other arithmetic, body(): jnp.zeros((experts * block_most, features), jnp.bfloat16).at[send_index]  6.33 us
    all_to_all x1, starting transfers between devices, body(): lax.all_to_all(send_rows, 'expert', split_axis=0, concat_axis=0, tiled=True)  4.72 us
    scatter x1, local copies, waits for them, and re-layouts, body(): jnp.full((experts * block_most,), capacity, jnp.int32).at[send_index]  4.32 us
  transfers between devices with their start and end apart: 3, of which 2 were waited for; matrix products, arithmetic and copies ran while one was open for 14% of the time, Pallas kernels for 0%

commit v1 on v0

v1 whole, which is shorter than its diff:
```python
import jax
import jax.numpy as jnp
from jax import lax
from jax.experimental import pallas as pl
from jax.experimental.pallas import tpu as pltpu
from jax.sharding import PartitionSpec as P

LANES = 256
PAIRS = 16
COUNT = 192


def dot(a, b, da=1, db=0):
    return lax.dot_general(a, b, (((da,), (db,)), ((), ())), preferred_element_type=jnp.float32)


def send_kernel(ids_ref, weights_ref, first_ref, own_ref, second_ref, out_ref):
    features, tokens = own_ref.shape
    experts = out_ref.shape[0]
    ids, weights = ids_ref[...], weights_ref[...]
    lane = lax.broadcasted_iota(jnp.int32, (tokens, 128), 1)
    named = (ids[:, 0:1] == lane) | (ids[:, 1:2] == lane)
    earlier = lax.broadcasted_iota(jnp.int32, (tokens, tokens), 1) < lax.broadcasted_iota(
        jnp.int32, (tokens, tokens), 0
    )
    member = jnp.where(named, 1.0, 0.0).astype(jnp.bfloat16)
    ranks = dot(jnp.where(earlier, 1.0, 0.0).astype(jnp.bfloat16), member).astype(jnp.int32)
    ranks = jnp.where(named, ranks, -1)
    place = lax.broadcasted_iota(jnp.int32, (tokens, LANES), 1)
    for e in range(experts):
        chosen = place == ranks[:, e : e + 1]
        weight = jnp.where(ids[:, 0:1] == e, weights[:, 0:1], weights[:, 1:2])
        scale = jnp.sum(jnp.where(chosen, weight, 0.0), axis=0, keepdims=True)
        count = jnp.sum(jnp.where(ranks[:, e : e + 1] >= 0, 1.0, 0.0), axis=0, keepdims=True)
        pick = jnp.where(chosen, 1.0, 0.0).astype(jnp.bfloat16)
        at_count = lax.broadcasted_iota(jnp.int32, (features, LANES), 1) == COUNT
        for part, ref in enumerate((first_ref, own_ref, second_ref)):
            rows = dot(ref[...], pick) * scale
            out_ref[e, part * features : (part + 1) * features, :] = jnp.where(
                at_count, count, rows
            ).astype(jnp.bfloat16)


def place_kernel(base_ref, rows_ref, a_ref, b_ref, sums_a, sums_b):
    sources, wide, _ = rows_ref.shape
    height, capacity = a_ref.shape
    span = sums_a.shape[1] - capacity
    low = wide - height
    sums_a[...] = jnp.zeros_like(sums_a)
    sums_b[...] = jnp.zeros_like(sums_b)
    rank = lax.broadcasted_iota(jnp.int32, (LANES, 1), 0)
    lane = lax.broadcasted_iota(jnp.int32, (LANES, span), 1)
    spare = lax.broadcasted_iota(jnp.int32, (16, 128), 1) == COUNT - 128

    def source(i, offset):
        counts = rows_ref[i, 0:16, 128:256].astype(jnp.float32)
        count = jnp.max(jnp.where(spare, counts, 0.0)).astype(jnp.int32)
        for base, sums, rows in (
            (base_ref[0], sums_a, rows_ref[i, 0:height, :]),
            (base_ref[1], sums_b, rows_ref[i, low:, :]),
        ):
            slot = offset - base
            slot = jnp.where(slot < 0, slot + capacity, slot)
            start = pl.multiple_of((slot // 128) * 128, 128)
            goal = jnp.where(rank < count, rank + (slot - start), -1)
            pick = jnp.where(goal == lane, 1.0, 0.0).astype(jnp.bfloat16)
            sums[:, pl.ds(start, span)] += dot(rows, pick)
        return offset + count

    lax.fori_loop(0, sources, source, jnp.int32(0))
    for sums, out in ((sums_a, a_ref), (sums_b, b_ref)):
        out[:, 0:span] = (sums[:, 0:span] + sums[:, capacity:]).astype(jnp.bfloat16)
        out[:, span:] = sums[:, span:capacity].astype(jnp.bfloat16)


def near_kernel(*refs):
    arranged, blocks, out, held = refs[0], refs[1:-2], refs[-2], refs[-1]
    size = blocks[0].shape[0]
    for i, block in enumerate(blocks):
        held[i * size : (i + 1) * size, :] = block[...]
    out[...] = dot(arranged[...], held[...])


def far_kernel(*refs):
    total, arranged, blocks, (top, bottom), held = refs[0], refs[1], refs[2:-3], refs[-3:-1], refs[-1]
    size = blocks[0].shape[0]
    for i, block in enumerate(blocks):
        held[i * size : (i + 1) * size, :] = block[...]
    half = top.shape[0]
    top[...] = (total[0:half, :] + dot(arranged[0:half, :], held[...])).astype(jnp.bfloat16)
    bottom[...] = (total[half:, :] + dot(arranged[half:, :], held[...])).astype(jnp.bfloat16)


def params(megabytes):
    return pltpu.CompilerParams(vmem_limit_bytes=megabytes << 20)


def cost(flops, bytes_accessed):
    return pl.CostEstimate(flops=flops, bytes_accessed=bytes_accessed, transcendentals=0)


def scaled_rows(out_grad, expert_ids, combine, grad_a, grad_b, experts):
    features, tokens = out_grad.shape
    wide = 3 * features
    return pl.pallas_call(
        send_kernel,
        out_shape=jax.ShapeDtypeStruct((experts, wide, LANES), jnp.bfloat16),
        compiler_params=params(12),
        cost_estimate=cost(2 * experts * LANES * tokens * wide, 6 << 20),
    )(expert_ids, combine, grad_a, out_grad, grad_b)


def place(rows, even, z, share, near, features, capacity):
    experts, wide, _ = rows.shape
    base_a = share * (jnp.where(even, z, z - 1) - 2 * near)
    base_b = share * (jnp.where(even, z - 1, z) - 2 * near)
    bases = jnp.stack([base_a % capacity, base_b % capacity]).astype(jnp.int32)
    return pl.pallas_call(
        place_kernel,
        out_shape=[jax.ShapeDtypeStruct((2 * features, capacity), jnp.bfloat16)] * 2,
        in_specs=[
            pl.BlockSpec(memory_space=pltpu.SMEM),
            pl.BlockSpec(memory_space=pltpu.VMEM),
        ],
        scratch_shapes=[
            pltpu.VMEM((2 * features, capacity + 384), jnp.float32),
            pltpu.VMEM((2 * features, capacity + 384), jnp.float32),
        ],
        compiler_params=params(16),
        cost_estimate=cost(8 * features * experts * LANES * 384, 6 << 20),
    )(bases, rows)


def after(value, chain, s):
    return lax.optimization_barrier((value, chain[s], chain[PAIRS - s]))[0]


def before(values, chain, s):
    *values, chain[s], chain[PAIRS - s] = lax.optimization_barrier(
        (*values, chain[s], chain[PAIRS - s])
    )
    return values


def near_product(chain, arranged, near):
    depth = arranged.shape[1] // 2
    blocks = [chain[(d - near) % PAIRS] for d in range(2 * near)]
    quarter = blocks[0].shape[1]
    return pl.pallas_call(
        near_kernel,
        out_shape=jax.ShapeDtypeStruct((arranged.shape[0], quarter), jnp.float32),
        scratch_shapes=[pltpu.VMEM((depth, quarter), jnp.bfloat16)],
        compiler_params=params(12),
        cost_estimate=cost(2 * arranged.shape[0] * depth * quarter, 4 << 20),
    )(arranged[:, :depth], *blocks)


def far_product(total, chain, arranged, near):
    depth = arranged.shape[1] // 2
    blocks = [chain[(d - near) % PAIRS] for d in range(2 * near, PAIRS)]
    quarter = blocks[0].shape[1]
    half = jax.ShapeDtypeStruct((arranged.shape[0] // 2, quarter), jnp.bfloat16)
    return pl.pallas_call(
        far_kernel,
        out_shape=[half, half],
        scratch_shapes=[pltpu.VMEM((depth, quarter), jnp.bfloat16)],
        compiler_params=params(12),
        cost_estimate=cost(2 * arranged.shape[0] * depth * quarter, 4 << 20),
    )(total, arranged[:, depth:], *blocks)


def body(out_grad, expert_ids, combine, hidden):
    planes = lax.axis_size("dp")
    experts = lax.axis_size("expert")
    out_grad = out_grad.T
    features = out_grad.shape[0]
    hidden = hidden[0]
    share, units = hidden.shape
    capacity = share * planes
    quarter = units // 4
    z = lax.axis_index("dp")
    even = z % 2 == 0

    swap_a = [(i, i ^ 1) for i in range(planes)]
    swap_b = [(i, ((i + 1) ^ 1) - 1) for i in range(planes)]
    swap_b = [(i, j % planes) for i, j in swap_b]
    right = [(i, (i + 2) % planes) for i in range(planes)]
    left = [(i, (i - 2) % planes) for i in range(planes)]

    q = [hidden[:, i * quarter : (i + 1) * quarter] for i in range(4)]
    keep_a, give_a = jnp.where(even, q[0], q[1]), jnp.where(even, q[1], q[0])
    keep_b, give_b = jnp.where(even, q[3], q[2]), jnp.where(even, q[2], q[3])
    got_a = lax.ppermute(give_a, "dp", swap_a)
    got_b = lax.ppermute(give_b, "dp", swap_b)
    grad_a = lax.ppermute(out_grad, "dp", swap_a)
    grad_b = lax.ppermute(out_grad, "dp", swap_b)
    block_a = jnp.concatenate([jnp.where(even, keep_a, got_a), jnp.where(even, got_a, keep_a)])
    block_b = jnp.concatenate([jnp.where(even, got_b, keep_b), jnp.where(even, keep_b, got_b)])

    chain_a, chain_b = {0: block_a}, {0: block_b}
    half = PAIRS // 2
    near = half // 2
    for s in range(1, half + 1):
        chain_a[PAIRS - s] = lax.ppermute(chain_a[(1 - s) % PAIRS], "dp", right)
        if s < half:
            chain_a[s] = lax.ppermute(chain_a[s - 1], "dp", left)
        if s == 2:
            ids = after(after(expert_ids, chain_a, 1), chain_b, 1)
            rows = scaled_rows(out_grad, ids, combine, grad_a, grad_b, experts)
            (rows,) = before([rows], chain_b, 1)
        if s == 3:
            rows = after(after(rows, chain_a, 2), chain_b, 2)
            rows = lax.all_to_all(rows, "expert", split_axis=0, concat_axis=0, tiled=True)
        if s == 6:
            rows = after(rows, chain_b, 5)
            arranged = place(rows, even, z, share, near, features, capacity)
            arranged = before(arranged, chain_b, 5)
        if s == 7:
            total_b = near_product(chain_b, after(arranged[1], chain_b, 6), near)
            (total_b,) = before([total_b], chain_b, 6)
        if s == 8:
            total_a = near_product(chain_a, after(arranged[0], chain_b, 7), near)
            (total_a,) = before([total_a], chain_b, 7)
            totals = total_a, total_b
        if s < half:
            chain_b[PAIRS - s] = lax.ppermute(chain_b[(1 - s) % PAIRS], "dp", right)
        chain_b[s] = lax.ppermute(chain_b[s - 1], "dp", left)

    results = [
        far_product(t, c, a, near) for t, c, a in zip(totals, (chain_a, chain_b), arranged)
    ]
    (theirs_a, mine_a), (mine_b, theirs_b) = results
    back_a = lax.ppermute(theirs_a, "dp", swap_a)
    back_b = lax.ppermute(theirs_b, "dp", swap_b)
    out = jnp.concatenate(
        [
            jnp.where(even, mine_a, back_a),
            jnp.where(even, back_a, mine_a),
            jnp.where(even, back_b, mine_b),
            jnp.where(even, mine_b, back_b),
        ],
        axis=1,
    )
    return out.T[None]


def solution(mesh):
    return jax.shard_map(
        body,
        mesh=mesh,
        in_specs=(
            P("expert", "dp"),
            P("expert", None),
            P("expert", None),
            P("expert", "dp", "tensor"),
        ),
        out_specs=P("expert", "tensor", "dp"),
        check_vma=False,
    )
```

time: 202 us -> 234 us (1.16)
  starting transfers between devices: 8.04 us -> 156 us
  waiting for transfers between devices: 132 us -> 50.4 us
  Pallas kernels: 0 us -> 17.2 us
  local copies, waits for them, and re-layouts: 19.1 us -> 3.21 us
  between operations: 14.2 us -> 0.75 us
  blocking collectives: 9.22 us -> 0 us
  matrix products: 8.38 us -> 0 us
  other arithmetic: 9.93 us -> 3.66 us
    ppermute x0 -> x36, starting transfers between devices: none -> 151 us  [the longest x8 33.6 us: body(): chain_b[s] = lax.ppermute(chain_b[s - 1], 'dp', left)]
    all_gather x1 -> x0, waiting for transfers between devices: 118 us -> none  [body(): lax.all_gather(hidden[0], 'dp', axis=0, tiled=True)]
    ppermute x0 -> x36, waiting for transfers between devices: none -> 50.3 us  [the longest x7 21.2 us: body(): chain_b[PAIRS - s] = lax.ppermute(chain_b[(1 - s) % PAIRS], 'dp', right)]
    pallas_call x0 -> x6, Pallas kernels: none -> 17.2 us  [the longest x1 5.55 us: place(): pl.pallas_call(place_kernel, out_shape=[jax.ShapeDtypeStruct((2 * feature...]
    all_to_all x2 -> x1, waiting for transfers between devices: 13 us -> 0.01 us  [body(): lax.all_to_all(rows, 'expert', split_axis=0, concat_axis=0, tiled=True)]
    scatter x2 -> x0, local copies, waits for them, and re-layouts: 11.8 us -> none  [the longest x1 7.47 us: body(): arranged.at[arrived_slots.reshape(-1)]]
    unnamed x1 -> x0, blocking collectives: 9.22 us -> none
    dot_general x1 -> x0, matrix products: 8.38 us -> none  [body(): lax.dot_general(lax.all_gather(hidden[0], 'dp', axis=0, tiled=True), arra...]
  transfers between devices with their start and end apart: 3 -> 37, of which waited for: 2 -> 13; matrix products, arithmetic and copies ran while one was open for 14% -> 0% of each run, Pallas kernels for 0% -> 7%
where the time goes in v1:
time: 234 us; the launch traced here: 231 us
  starting transfers between devices  156 us (67%)
  waiting for transfers between devices  50.4 us (22%)
  Pallas kernels  17.2 us (7%)
  other arithmetic  3.66 us (2%)
  local copies, waits for them, and re-layouts  3.21 us (1%)
    ppermute x8, starting transfers between devices, body(): chain_b[s] = lax.ppermute(chain_b[s - 1], 'dp', left)  33.6 us
    ppermute x7, starting transfers between devices, body(): chain_a[s] = lax.ppermute(chain_a[s - 1], 'dp', left)  32.1 us
    ppermute x8, starting transfers between devices, body(): chain_a[PAIRS - s] = lax.ppermute(chain_a[(1 - s) % PAIRS], 'dp', right)  22.6 us
    ppermute x7, waiting for transfers between devices, body(): chain_b[PAIRS - s] = lax.ppermute(chain_b[(1 - s) % PAIRS], 'dp', right)  21.2 us
    ppermute x7, starting transfers between devices, body(): chain_b[PAIRS - s] = lax.ppermute(chain_b[(1 - s) % PAIRS], 'dp', right)  19.9 us
    ppermute x1, starting transfers between devices, body(): got_b = lax.ppermute(give_b, 'dp', swap_b)  18.7 us
    ppermute x1, starting transfers between devices, body(): back_b = lax.ppermute(theirs_b, 'dp', swap_b)  12.4 us
    ppermute x8, waiting for transfers between devices, body(): chain_b[s] = lax.ppermute(chain_b[s - 1], 'dp', left)  12.3 us
  transfers between devices with their start and end apart: 37, of which 13 were waited for; matrix products, arithmetic and copies ran while one was open for 0% of the time, Pallas kernels for 7%

profile of v1, /device:TPU:24, one launch (start us, length us, event | category | flops | bytes accessed | tf_op | source)
XLA Modules:
  0.0 230.9 jit_solution(15767377371511263173)
XLA Ops:
  0.0 1.1 broadcast_select_fusion.7
  1.1 18.7 %collective-permute-start.3 = (bf16[48,1024]{1,0:T(8,128)(2,1)S(1)}, bf16[48,1024]{1,0:T(8,128)(2,1)S(1)}, u32[]{:S(2)}, u32[]{:S(2)}) collective-permute-start(bf16[48,1024]{1,0:T(8,128)(2,1)S(1)} %get-tuple-element.67), channel_id=1, source_target_pairs={{0,992},{32,64},{64,32},{96,128},{128,96},{160,192},{192,160},{224... | collective-permute-start | bytes 294920 | tf_op jit(solution)/shard_map/ppermute | solution.py:194
  19.8 1.9 collective-permute-start
  21.7 0.8 collective-permute-done.3
  22.6 3.7 %collective-permute-done = bf16[48,1024]{1,0:T(8,128)(2,1)S(1)} collective-permute-done((bf16[48,1024]{1,0:T(8,128)(2,1)S(1)}, bf16[48,1024]{1,0:T(8,128)(2,1)S(1)}, u32[]{:S(2)}, u32[]{:S(2)}) %collective-permute-start) | collective-permute-done | bytes 98336 | tf_op jit(solution)/shard_map/ppermute | solution.py:193
  26.3 1.1 broadcast_select_fusion.5
  27.4 3.4 %collective-permute-start.1 = (bf16[96,1024]{1,0:T(8,128)(2,1)S(1)}, bf16[96,1024]{1,0:T(8,128)(2,1)S(1)}, u32[]{:S(2)}, u32[]{:S(2)}) collective-permute-start(bf16[96,1024]{1,0:T(8,128)(2,1)S(1)} %pad_maximum_fusion.refs_5_), channel_id=1, source_target_pairs={{0,960},{32,992},{64,0},{96,32},{128,64},{160,96},{192,128},{224,1... | collective-permute-start | bytes 589832 | tf_op jit(solution)/shard_map/ppermute | solution.py:206
  30.8 3.4 %collective-permute-start.2 = (bf16[96,1024]{1,0:T(8,128)(2,1)S(1)}, bf16[96,1024]{1,0:T(8,128)(2,1)S(1)}, u32[]{:S(2)}, u32[]{:S(2)}) collective-permute-start(bf16[96,1024]{1,0:T(8,128)(2,1)S(1)} %pad_maximum_fusion.refs_5_), channel_id=1, source_target_pairs={{0,64},{32,96},{64,128},{96,160},{128,192},{160,224},{192,256},{22... | collective-permute-start | bytes 589832 | tf_op jit(solution)/shard_map/ppermute | solution.py:204
  34.2 4.6 %collective-permute-start.4 = (bf16[96,1024]{1,0:T(8,128)(2,1)S(1)}, bf16[96,1024]{1,0:T(8,128)(2,1)S(1)}, u32[]{:S(2)}, u32[]{:S(2)}) collective-permute-start(bf16[96,1024]{1,0:T(8,128)(2,1)S(1)} %pad_maximum_fusion.1.refs_5_), channel_id=1, source_target_pairs={{0,960},{32,992},{64,0},{96,32},{128,64},{160,96},{192,128},{224,1... | collective-permute-start | bytes 589832 | tf_op jit(solution)/shard_map/ppermute | solution.py:227
  38.8 2.2 collective-permute-start.5
  41.0 1.9 collective-permute-start.6
  42.9 1.0 collective-permute-done.1.refs_6_
  43.9 5.3 %collective-permute-start.7 = (bf16[192,512]{1,0:T(8,128)(2,1)S(1)}, bf16[192,512]{1,0:T(8,128)(2,1)S(1)}, u32[]{:S(2)}, u32[]{:S(2)}) collective-permute-start(bf16[192,512]{1,0:T(8,128)(2,1)S(1)} %bitcast.9), channel_id=1, source_target_pairs={{0,992},{32,64},{64,32},{96,128},{128,96},{160,192},{192,160},{224... | collective-permute-start | bytes 589832 | tf_op jit(solution)/shard_map/ppermute | solution.py:196
  49.3 0.1 copy.6.weights_ref
  49.4 4.7 %collective-permute-done.5.refs_4_ = bf16[96,1024]{1,0:T(8,128)(2,1)S(1)} collective-permute-done((bf16[96,1024]{1,0:T(8,128)(2,1)S(1)}, bf16[96,1024]{1,0:T(8,128)(2,1)S(1)}, u32[]{:S(2)}, u32[]{:S(2)}) %collective-permute-start.5) | collective-permute-done | bytes 196640 | tf_op jit(solution)/shard_map/ppermute | solution.py:226
  54.3 2.6 %collective-permute-start.8 = (bf16[96,1024]{1,0:T(8,128)(2,1)S(1)}, bf16[96,1024]{1,0:T(8,128)(2,1)S(1)}, u32[]{:S(2)}, u32[]{:S(2)}) collective-permute-start(bf16[96,1024]{1,0:T(8,128)(2,1)S(1)} %collective-permute-done.1.refs_6_), channel_id=1, source_target_pairs={{0,960},{32,992},{64,0},{96,32},{128,64},{160,96},{192,128},{224,1... | collective-permute-start | bytes 589832 | tf_op jit(solution)/shard_map/ppermute | solution.py:206
  57.0 4.1 %collective-permute-start.9 = (bf16[96,1024]{1,0:T(8,128)(2,1)S(1)}, bf16[96,1024]{1,0:T(8,128)(2,1)S(1)}, u32[]{:S(2)}, u32[]{:S(2)}) collective-permute-start(bf16[96,1024]{1,0:T(8,128)(2,1)S(1)} %collective-permute-done.2.refs_4_), channel_id=1, source_target_pairs={{0,64},{32,96},{64,128},{96,160},{128,192},{160,224},{192,256},{22... | collective-permute-start | bytes 589832 | tf_op jit(solution)/shard_map/ppermute | solution.py:204
  61.1 4.1 %shard_map.46 = bf16[8,576,256]{2,1,0:T(8,128)(2,1)} custom-call(s32[512,2]{1,0:T(8,128)S(1)} %copy.5.ids_ref, f32[512,2]{1,0:T(8,128)S(1)} %copy.6.weights_ref, bf16[192,512]{1,0:T(8,128)(2,1)S(1)} %collective-permute-done.6.first_ref, bf16[192,512]{1,0:T(8,128)(2,1)S(1)} %bitcast.10, bf16[192,512]{1,0:T(8,128)(2,1)S(1)} %collective-permute-done.7.second_ref), custom_call_target="tpu_custom_call" | custom-call | flops 1207959552 | bytes 6291456 | tf_op jit(solution)/shard_map/pallas_call | solution.py:105
  65.2 3.8 %collective-permute-start.10 = (bf16[96,1024]{1,0:T(8,128)(2,1)S(1)}, bf16[96,1024]{1,0:T(8,128)(2,1)S(1)}, u32[]{:S(2)}, u32[]{:S(2)}) collective-permute-start(bf16[96,1024]{1,0:T(8,128)(2,1)S(1)} %collective-permute-done.4.refs_6_), channel_id=1, source_target_pairs={{0,960},{32,992},{64,0},{96,32},{128,64},{160,96},{192,128},{224,1... | collective-permute-start | bytes 589832 | tf_op jit(solution)/shard_map/ppermute | solution.py:227
  69.1 2.9 %collective-permute-start.11 = (bf16[96,1024]{1,0:T(8,128)(2,1)S(1)}, bf16[96,1024]{1,0:T(8,128)(2,1)}, u32[]{:S(2)}, u32[]{:S(2)}) collective-permute-start(bf16[96,1024]{1,0:T(8,128)(2,1)S(1)} %collective-permute-done.5.refs_4_), channel_id=1, source_target_pairs={{0,64},{32,96},{64,128},{96,160},{128,192},{160,224},{192,256},{22... | collective-permute-start | bytes 589832 | tf_op jit(solution)/shard_map/ppermute | solution.py:226
  72.0 2.1 collective-permute-done.10.refs_7_
  74.1 0.7 copy-done.6
  74.8 6.0 %collective-permute-done.11.refs_3_ = bf16[96,1024]{1,0:T(8,128)(2,1)} collective-permute-done((bf16[96,1024]{1,0:T(8,128)(2,1)S(1)}, bf16[96,1024]{1,0:T(8,128)(2,1)}, u32[]{:S(2)}, u32[]{:S(2)}) %collective-permute-start.11) | collective-permute-done | bytes 196640 | tf_op jit(solution)/shard_map/ppermute | solution.py:226
  80.8 4.3 %all-to-all-start = ((bf16[8,576,256]{2,1,0:T(8,128)(2,1)}), bf16[8,576,256]{2,1,0:T(8,128)(2,1)S(1)}, u32[]{:S(2)}, u32[]{:S(2)}) async-start(bf16[8,576,256]{2,1,0:T(8,128)(2,1)} %shard_map.46), calls=%async_computation | async-start | bytes 4718592 | tf_op jit(solution)/shard_map/all_to_all | solution.py:213
  85.1 2.1 collective-permute-start.22
  87.2 5.8 %collective-permute-start.12 = (bf16[96,1024]{1,0:T(8,128)(2,1)}, bf16[96,1024]{1,0:T(8,128)(2,1)S(1)}, u32[]{:S(2)}, u32[]{:S(2)}) collective-permute-start(bf16[96,1024]{1,0:T(8,128)(2,1)} %copy-done.6), channel_id=1, source_target_pairs={{0,960},{32,992},{64,0},{96,32},{128,64},{160,96},{192,128},{224,1... | collective-permute-start | bytes 589832 | tf_op jit(solution)/shard_map/ppermute | solution.py:227
  93.0 1.9 collective-permute-start.15
  94.9 6.0 %collective-permute-start.24 = (bf16[96,1024]{1,0:T(8,128)(2,1)S(1)}, bf16[96,1024]{1,0:T(8,128)(2,1)}, u32[]{:S(2)}, u32[]{:S(2)}) collective-permute-start(bf16[96,1024]{1,0:T(8,128)(2,1)S(1)} %collective-permute-done.8.refs_7_), channel_id=1, source_target_pairs={{0,960},{32,992},{64,0},{96,32},{128,64},{160,96},{192,128},{224,1... | collective-permute-start | bytes 589832 | tf_op jit(solution)/shard_map/ppermute | solution.py:206
  101.0 1.9 collective-permute-start.23
  102.9 0.7 copy-done.4
  103.6 6.0 %collective-permute-start.13 = (bf16[96,1024]{1,0:T(8,128)(2,1)S(1)}, bf16[96,1024]{1,0:T(8,128)(2,1)}, u32[]{:S(2)}, u32[]{:S(2)}) collective-permute-start(bf16[96,1024]{1,0:T(8,128)(2,1)S(1)} %collective-permute-done.12.refs_8_), channel_id=1, source_target_pairs={{0,960},{32,992},{64,0},{96,32},{128,64},{160,96},{192,128},{224,1... | collective-permute-start | bytes 589832 | tf_op jit(solution)/shard_map/ppermute | solution.py:227
  109.7 0.7 copy-done.8
  110.3 1.9 collective-permute-start.16
  112.3 0.7 copy-done.10
  112.9 6.0 %collective-permute-start.25 = (bf16[96,1024]{1,0:T(8,128)(2,1)}, bf16[96,1024]{1,0:T(8,128)(2,1)}, u32[]{:S(2)}, u32[]{:S(2)}) collective-permute-start(bf16[96,1024]{1,0:T(8,128)(2,1)} %collective-permute-done.24.refs_8_), channel_id=1, source_target_pairs={{0,960},{32,992},{64,0},{96,32},{128,64},{160,96},{192,128},{224,1... | collective-permute-start | bytes 589832 | tf_op jit(solution)/shard_map/ppermute | solution.py:206
  119.0 1.9 collective-permute-start.29
  120.9 6.0 %collective-permute-start.14 = (bf16[96,1024]{1,0:T(8,128)(2,1)}, bf16[96,1024]{1,0:T(8,128)(2,1)}, u32[]{:S(2)}, u32[]{:S(2)}) collective-permute-start(bf16[96,1024]{1,0:T(8,128)(2,1)} %collective-permute-done.13.refs_2_), channel_id=1, source_target_pairs={{0,960},{32,992},{64,0},{96,32},{128,64},{160,96},{192,128},{224,1... | collective-permute-start | bytes 589832 | tf_op jit(solution)/shard_map/ppermute | solution.py:227
  127.0 1.9 collective-permute-start.17
  129.0 7.1 %collective-permute-start.26 = (bf16[96,1024]{1,0:T(8,128)(2,1)}, bf16[96,1024]{1,0:T(8,128)(2,1)}, u32[]{:S(2)}, u32[]{:S(2)}) collective-permute-start(bf16[96,1024]{1,0:T(8,128)(2,1)} %collective-permute-done.25.refs_2_), channel_id=1, source_target_pairs={{0,960},{32,992},{64,0},{96,32},{128,64},{160,96},{192,128},{224,1... | collective-permute-start | bytes 589832 | tf_op jit(solution)/shard_map/ppermute | solution.py:206
  136.2 0.8 collective-permute-done.29.refs_9_
  137.0 2.6 %collective-permute-start.30 = (bf16[96,1024]{1,0:T(8,128)(2,1)}, bf16[96,1024]{1,0:T(8,128)(2,1)}, u32[]{:S(2)}, u32[]{:S(2)}) collective-permute-start(bf16[96,1024]{1,0:T(8,128)(2,1)} %collective-permute-done.29.refs_9_), channel_id=1, source_target_pairs={{0,64},{32,96},{64,128},{96,160},{128,192},{160,224},{192,256},{22... | collective-permute-start | bytes 589832 | tf_op jit(solution)/shard_map/ppermute | solution.py:204
  139.6 6.0 %collective-permute-done.17.refs_9_ = bf16[96,1024]{1,0:T(8,128)(2,1)} collective-permute-done((bf16[96,1024]{1,0:T(8,128)(2,1)}, bf16[96,1024]{1,0:T(8,128)(2,1)}, u32[]{:S(2)}, u32[]{:S(2)}) %collective-permute-start.17) | collective-permute-done | bytes 196640 | tf_op jit(solution)/shard_map/ppermute | solution.py:226
  145.6 5.5 %shard_map.47 = (bf16[384,1536]{1,0:T(8,128)(2,1)S(1)}, bf16[384,1536]{1,0:T(8,128)(2,1)S(1)}) custom-call(s32[2]{0:T(128)S(1)} %pad_add_fusion.base_ref, bf16[8,576,256]{2,1,0:T(8,128)(2,1)S(1)} %all-to-all-done.rows_ref), custom_call_target="tpu_custom_call" | custom-call | flops 1207959552 | bytes 6291456 | tf_op jit(solution)/shard_map/pallas_call | solution.py:118
  151.1 2.5 %collective-permute-start.18 = (bf16[96,1024]{1,0:T(8,128)(2,1)}, bf16[96,1024]{1,0:T(8,128)(2,1)S(1)}, u32[]{:S(2)}, u32[]{:S(2)}) collective-permute-start(bf16[96,1024]{1,0:T(8,128)(2,1)} %collective-permute-done.14.refs_3_), channel_id=1, source_target_pairs={{0,960},{32,992},{64,0},{96,32},{128,64},{160,96},{192,128},{224,1... | collective-permute-start | bytes 589832 | tf_op jit(solution)/shard_map/ppermute | solution.py:227
  153.6 4.3 %collective-permute-start.19 = (bf16[96,1024]{1,0:T(8,128)(2,1)}, bf16[96,1024]{1,0:T(8,128)(2,1)S(1)}, u32[]{:S(2)}, u32[]{:S(2)}) collective-permute-start(bf16[96,1024]{1,0:T(8,128)(2,1)} %collective-permute-done.17.refs_9_), channel_id=1, source_target_pairs={{0,64},{32,96},{64,128},{96,160},{128,192},{160,224},{192,256},{22... | collective-permute-start | bytes 589832 | tf_op jit(solution)/shard_map/ppermute | solution.py:226
  157.9 3.7 %collective-permute-start.27 = (bf16[96,1024]{1,0:T(8,128)(2,1)}, bf16[96,1024]{1,0:T(8,128)(2,1)S(1)}, u32[]{:S(2)}, u32[]{:S(2)}) collective-permute-start(bf16[96,1024]{1,0:T(8,128)(2,1)} %collective-permute-done.26.refs_3_), channel_id=1, source_target_pairs={{0,960},{32,992},{64,0},{96,32},{128,64},{160,96},{192,128},{224,1... | collective-permute-start | bytes 589832 | tf_op jit(solution)/shard_map/ppermute | solution.py:206
  161.6 3.0 %collective-permute-start.31 = (bf16[96,1024]{1,0:T(8,128)(2,1)}, bf16[96,1024]{1,0:T(8,128)(2,1)S(1)}, u32[]{:S(2)}, u32[]{:S(2)}) collective-permute-start(bf16[96,1024]{1,0:T(8,128)(2,1)} %collective-permute-done.30.refs_8_), channel_id=1, source_target_pairs={{0,64},{32,96},{64,128},{96,160},{128,192},{160,224},{192,256},{22... | collective-permute-start | bytes 589832 | tf_op jit(solution)/shard_map/ppermute | solution.py:204
  164.7 4.2 %collective-permute-done.18.refs_4_ = bf16[96,1024]{1,0:T(8,128)(2,1)S(1)} collective-permute-done((bf16[96,1024]{1,0:T(8,128)(2,1)}, bf16[96,1024]{1,0:T(8,128)(2,1)S(1)}, u32[]{:S(2)}, u32[]{:S(2)}) %collective-permute-start.18) | collective-permute-done | bytes 196640 | tf_op jit(solution)/shard_map/ppermute | solution.py:227
  168.9 1.8 shard_map.48.refs_0_
  170.7 2.1 collective-permute-start.20
  172.8 4.8 %collective-permute-start.21 = (bf16[96,1024]{1,0:T(8,128)(2,1)S(1)}, bf16[96,1024]{1,0:T(8,128)(2,1)S(1)}, u32[]{:S(2)}, u32[]{:S(2)}) collective-permute-start(bf16[96,1024]{1,0:T(8,128)(2,1)S(1)} %collective-permute-done.19.refs_8_), channel_id=1, source_target_pairs={{0,64},{32,96},{64,128},{96,160},{128,192},{160,224},{192,256},{22... | collective-permute-start | bytes 589832 | tf_op jit(solution)/shard_map/ppermute | solution.py:226
  177.6 3.2 %collective-permute-start.28 = (bf16[96,1024]{1,0:T(8,128)(2,1)S(1)}, bf16[96,1024]{1,0:T(8,128)(2,1)S(1)}, u32[]{:S(2)}, u32[]{:S(2)}) collective-permute-start(bf16[96,1024]{1,0:T(8,128)(2,1)S(1)} %collective-permute-done.27.refs_4_), channel_id=1, source_target_pairs={{0,960},{32,992},{64,0},{96,32},{128,64},{160,96},{192,128},{224,1... | collective-permute-start | bytes 589832 | tf_op jit(solution)/shard_map/ppermute | solution.py:206
  180.8 3.6 %collective-permute-start.32 = (bf16[96,1024]{1,0:T(8,128)(2,1)S(1)}, bf16[96,1024]{1,0:T(8,128)(2,1)S(1)}, u32[]{:S(2)}, u32[]{:S(2)}) collective-permute-start(bf16[96,1024]{1,0:T(8,128)(2,1)S(1)} %collective-permute-done.31.refs_7_), channel_id=1, source_target_pairs={{0,64},{32,96},{64,128},{96,160},{128,192},{160,224},{192,256},{22... | collective-permute-start | bytes 589832 | tf_op jit(solution)/shard_map/ppermute | solution.py:204
  184.5 4.5 %collective-permute-done.21.refs_7_ = bf16[96,1024]{1,0:T(8,128)(2,1)S(1)} collective-permute-done((bf16[96,1024]{1,0:T(8,128)(2,1)S(1)}, bf16[96,1024]{1,0:T(8,128)(2,1)S(1)}, u32[]{:S(2)}, u32[]{:S(2)}) %collective-permute-start.21) | collective-permute-done | bytes 196640 | tf_op jit(solution)/shard_map/ppermute | solution.py:226
  189.0 1.8 shard_map.49.refs_0_
  190.8 4.2 %collective-permute-done.32.refs_6_ = bf16[96,1024]{1,0:T(8,128)(2,1)S(1)} collective-permute-done((bf16[96,1024]{1,0:T(8,128)(2,1)S(1)}, bf16[96,1024]{1,0:T(8,128)(2,1)S(1)}, u32[]{:S(2)}, u32[]{:S(2)}) %collective-permute-start.32) | collective-permute-done | bytes 196640 | tf_op jit(solution)/shard_map/ppermute | solution.py:204
  195.0 2.0 shard_map.50
  197.1 3.1 %collective-permute-start.33 = (bf16[192,1024]{1,0:T(8,128)(2,1)S(1)}, bf16[192,1024]{1,0:T(8,128)(2,1)S(1)}, u32[]{:S(2)}, u32[]{:S(2)}) collective-permute-start(bf16[192,1024]{1,0:T(8,128)(2,1)S(1)} %get-tuple-element.51), channel_id=1, source_target_pairs={{0,32},{32,0},{64,96},{96,64},{128,160},{160,128},{192,224},{224,1... | collective-permute-start | bytes 1179656 | tf_op jit(solution)/shard_map/ppermute | solution.py:233
  200.2 2.7 %collective-permute-start.34 = (bf16[96,1024]{1,0:T(8,128)(2,1)S(1)}, bf16[96,1024]{1,0:T(8,128)(2,1)S(1)}, u32[]{:S(2)}, u32[]{:S(2)}) collective-permute-start(bf16[96,1024]{1,0:T(8,128)(2,1)S(1)} %collective-permute-done.20.refs_5_), channel_id=1, source_target_pairs={{0,960},{32,992},{64,0},{96,32},{128,64},{160,96},{192,128},{224,1... | collective-permute-start | bytes 589832 | tf_op jit(solution)/shard_map/ppermute | solution.py:227
  203.0 6.0 %collective-permute-done.34.refs_6_ = bf16[96,1024]{1,0:T(8,128)(2,1)S(1)} collective-permute-done((bf16[96,1024]{1,0:T(8,128)(2,1)S(1)}, bf16[96,1024]{1,0:T(8,128)(2,1)S(1)}, u32[]{:S(2)}, u32[]{:S(2)}) %collective-permute-start.34) | collective-permute-done | bytes 196640 | tf_op jit(solution)/shard_map/ppermute | solution.py:227
  208.9 1.9 shard_map.51
  210.8 12.4 %collective-permute-start.35 = (bf16[192,1024]{1,0:T(8,128)(2,1)S(1)}, bf16[192,1024]{1,0:T(8,128)(2,1)S(1)}, u32[]{:S(2)}, u32[]{:S(2)}) collective-permute-start(bf16[192,1024]{1,0:T(8,128)(2,1)S(1)} %get-tuple-element.55), channel_id=1, source_target_pairs={{0,992},{32,64},{64,32},{96,128},{128,96},{160,192},{192,160},{224... | collective-permute-start | bytes 1179656 | tf_op jit(solution)/shard_map/ppermute | solution.py:234
  223.3 6.3 %collective-permute-done.35 = bf16[192,1024]{1,0:T(8,128)(2,1)S(1)} collective-permute-done((bf16[192,1024]{1,0:T(8,128)(2,1)S(1)}, bf16[192,1024]{1,0:T(8,128)(2,1)S(1)}, u32[]{:S(2)}, u32[]{:S(2)}) %collective-permute-start.35) | collective-permute-done | bytes 393248 | tf_op jit(solution)/shard_map/ppermute | solution.py:234
  229.6 1.3 maximum_bitcast_fusion
  (60 shorter events, 0.6 us)
Async XLA Ops:
  0.0 41.0 %copy-start.12 = (bf16[512,192]{0,1:T(8,128)(2,1)S(1)}, bf16[512,192]{0,1:T(8,128)(2,1)}, u32[]{:S(2)}) copy-start(bf16[512,192]{0,1:T(8,128)(2,1)} %param.4) | copy-start | bytes 589828
  0.0 49.3 %copy-start.13 = (f32[512,2]{0,1:T(2,128)S(1)}, f32[512,2]{0,1:T(2,128)}, u32[]{:S(2)}) copy-start(f32[512,2]{0,1:T(2,128)} %param.6) | copy-start | bytes 12292
  0.0 54.2 %copy-start.14 = (s32[512,2]{0,1:T(2,128)S(1)}, s32[512,2]{0,1:T(2,128)}, u32[]{:S(2)}) copy-start(s32[512,2]{0,1:T(2,128)} %param.5) | copy-start | bytes 12292
  1.1 21.5 %collective-permute-start.3 = (bf16[48,1024]{1,0:T(8,128)(2,1)S(1)}, bf16[48,1024]{1,0:T(8,128)(2,1)S(1)}, u32[]{:S(2)}, u32[]{:S(2)}) collective-permute-start(bf16[48,1024]{1,0:T(8,128)(2,1)S(1)} %get-tuple-element.67), channel_id=1, source_target_pairs={{0,992},{32,64},{64,32},{96,128},{128,96},{160,192},{192,160},{224... | collective-permute-start | bytes 294920 | tf_op jit(solution)/shard_map/ppermute | solution.py:194
  19.8 6.5 %collective-permute-start = (bf16[48,1024]{1,0:T(8,128)(2,1)S(1)}, bf16[48,1024]{1,0:T(8,128)(2,1)S(1)}, u32[]{:S(2)}, u32[]{:S(2)}) collective-permute-start(bf16[48,1024]{1,0:T(8,128)(2,1)S(1)} %get-tuple-element.68), channel_id=1, source_target_pairs={{0,32},{32,0},{64,96},{96,64},{128,160},{160,128},{192,224},{224,1... | collective-permute-start | bytes 294920 | tf_op jit(solution)/shard_map/ppermute | solution.py:193
  27.4 16.5 %collective-permute-start.1 = (bf16[96,1024]{1,0:T(8,128)(2,1)S(1)}, bf16[96,1024]{1,0:T(8,128)(2,1)S(1)}, u32[]{:S(2)}, u32[]{:S(2)}) collective-permute-start(bf16[96,1024]{1,0:T(8,128)(2,1)S(1)} %pad_maximum_fusion.refs_5_), channel_id=1, source_target_pairs={{0,960},{32,992},{64,0},{96,32},{128,64},{160,96},{192,128},{224,1... | collective-permute-start | bytes 589832 | tf_op jit(solution)/shard_map/ppermute | solution.py:206
  30.8 18.6 %collective-permute-start.2 = (bf16[96,1024]{1,0:T(8,128)(2,1)S(1)}, bf16[96,1024]{1,0:T(8,128)(2,1)S(1)}, u32[]{:S(2)}, u32[]{:S(2)}) collective-permute-start(bf16[96,1024]{1,0:T(8,128)(2,1)S(1)} %pad_maximum_fusion.refs_5_), channel_id=1, source_target_pairs={{0,64},{32,96},{64,128},{96,160},{128,192},{160,224},{192,256},{22... | collective-permute-start | bytes 589832 | tf_op jit(solution)/shard_map/ppermute | solution.py:204
  34.2 15.2 %collective-permute-start.4 = (bf16[96,1024]{1,0:T(8,128)(2,1)S(1)}, bf16[96,1024]{1,0:T(8,128)(2,1)S(1)}, u32[]{:S(2)}, u32[]{:S(2)}) collective-permute-start(bf16[96,1024]{1,0:T(8,128)(2,1)S(1)} %pad_maximum_fusion.1.refs_5_), channel_id=1, source_target_pairs={{0,960},{32,992},{64,0},{96,32},{128,64},{160,96},{192,128},{224,1... | collective-permute-start | bytes 589832 | tf_op jit(solution)/shard_map/ppermute | solution.py:227
  38.8 15.4 %collective-permute-start.5 = (bf16[96,1024]{1,0:T(8,128)(2,1)S(1)}, bf16[96,1024]{1,0:T(8,128)(2,1)S(1)}, u32[]{:S(2)}, u32[]{:S(2)}) collective-permute-start(bf16[96,1024]{1,0:T(8,128)(2,1)S(1)} %pad_maximum_fusion.1.refs_5_), channel_id=1, source_target_pairs={{0,64},{32,96},{64,128},{96,160},{128,192},{160,224},{192,256},{22... | collective-permute-start | bytes 589832 | tf_op jit(solution)/shard_map/ppermute | solution.py:226
  41.0 20.1 %collective-permute-start.6 = (bf16[192,512]{1,0:T(8,128)(2,1)S(1)}, bf16[192,512]{1,0:T(8,128)(2,1)S(1)}, u32[]{:S(2)}, u32[]{:S(2)}) collective-permute-start(bf16[192,512]{1,0:T(8,128)(2,1)S(1)} %bitcast.8), channel_id=1, source_target_pairs={{0,32},{32,0},{64,96},{96,64},{128,160},{160,128},{192,224},{224,1... | collective-permute-start | bytes 589832 | tf_op jit(solution)/shard_map/ppermute | solution.py:195
  43.9 17.2 %collective-permute-start.7 = (bf16[192,512]{1,0:T(8,128)(2,1)S(1)}, bf16[192,512]{1,0:T(8,128)(2,1)S(1)}, u32[]{:S(2)}, u32[]{:S(2)}) collective-permute-start(bf16[192,512]{1,0:T(8,128)(2,1)S(1)} %bitcast.9), channel_id=1, source_target_pairs={{0,992},{32,64},{64,32},{96,128},{128,96},{160,192},{192,160},{224... | collective-permute-start | bytes 589832 | tf_op jit(solution)/shard_map/ppermute | solution.py:196
  49.4 15.8 %copy-start = (bf16[96,1024]{1,0:T(8,128)(2,1)}, bf16[96,1024]{1,0:T(8,128)(2,1)S(1)}, u32[]{:S(2)}) copy-start(bf16[96,1024]{1,0:T(8,128)(2,1)S(1)} %collective-permute-done.4.refs_6_) | copy-start | bytes 589828
  54.2 14.9 %copy-start.2 = (bf16[96,1024]{1,0:T(8,128)(2,1)}, bf16[96,1024]{1,0:T(8,128)(2,1)S(1)}, u32[]{:S(2)}) copy-start(bf16[96,1024]{1,0:T(8,128)(2,1)S(1)} %collective-permute-done.5.refs_4_) | copy-start | bytes 589828
  54.3 17.6 %collective-permute-start.8 = (bf16[96,1024]{1,0:T(8,128)(2,1)S(1)}, bf16[96,1024]{1,0:T(8,128)(2,1)S(1)}, u32[]{:S(2)}, u32[]{:S(2)}) collective-permute-start(bf16[96,1024]{1,0:T(8,128)(2,1)S(1)} %collective-permute-done.1.refs_6_), channel_id=1, source_target_pairs={{0,960},{32,992},{64,0},{96,32},{128,64},{160,96},{192,128},{224,1... | collective-permute-start | bytes 589832 | tf_op jit(solution)/shard_map/ppermute | solution.py:206
  57.0 15.0 %collective-permute-start.9 = (bf16[96,1024]{1,0:T(8,128)(2,1)S(1)}, bf16[96,1024]{1,0:T(8,128)(2,1)S(1)}, u32[]{:S(2)}, u32[]{:S(2)}) collective-permute-start(bf16[96,1024]{1,0:T(8,128)(2,1)S(1)} %collective-permute-done.2.refs_4_), channel_id=1, source_target_pairs={{0,64},{32,96},{64,128},{96,160},{128,192},{160,224},{192,256},{22... | collective-permute-start | bytes 589832 | tf_op jit(solution)/shard_map/ppermute | solution.py:204
  65.2 8.9 %collective-permute-start.10 = (bf16[96,1024]{1,0:T(8,128)(2,1)S(1)}, bf16[96,1024]{1,0:T(8,128)(2,1)S(1)}, u32[]{:S(2)}, u32[]{:S(2)}) collective-permute-start(bf16[96,1024]{1,0:T(8,128)(2,1)S(1)} %collective-permute-done.4.refs_6_), channel_id=1, source_target_pairs={{0,960},{32,992},{64,0},{96,32},{128,64},{160,96},{192,128},{224,1... | collective-permute-start | bytes 589832 | tf_op jit(solution)/shard_map/ppermute | solution.py:227
  69.1 11.7 %collective-permute-start.11 = (bf16[96,1024]{1,0:T(8,128)(2,1)S(1)}, bf16[96,1024]{1,0:T(8,128)(2,1)}, u32[]{:S(2)}, u32[]{:S(2)}) collective-permute-start(bf16[96,1024]{1,0:T(8,128)(2,1)S(1)} %collective-permute-done.5.refs_4_), channel_id=1, source_target_pairs={{0,64},{32,96},{64,128},{96,160},{128,192},{160,224},{192,256},{22... | collective-permute-start | bytes 589832 | tf_op jit(solution)/shard_map/ppermute | solution.py:226
  74.1 0.7 copy-start.6
  80.8 64.8 %all-to-all-start = ((bf16[8,576,256]{2,1,0:T(8,128)(2,1)}), bf16[8,576,256]{2,1,0:T(8,128)(2,1)S(1)}, u32[]{:S(2)}, u32[]{:S(2)}) async-start(bf16[8,576,256]{2,1,0:T(8,128)(2,1)} %shard_map.46), calls=%async_computation | async-start | bytes 4718592 | tf_op jit(solution)/shard_map/all_to_all | solution.py:213
  85.1 15.9 %collective-permute-start.22 = (bf16[96,1024]{1,0:T(8,128)(2,1)S(1)}, bf16[96,1024]{1,0:T(8,128)(2,1)S(1)}, u32[]{:S(2)}, u32[]{:S(2)}) collective-permute-start(bf16[96,1024]{1,0:T(8,128)(2,1)S(1)} %collective-permute-done.9.refs_3_), channel_id=1, source_target_pairs={{0,64},{32,96},{64,128},{96,160},{128,192},{160,224},{192,256},{22... | collective-permute-start | bytes 589832 | tf_op jit(solution)/shard_map/ppermute | solution.py:204
  87.2 16.4 %collective-permute-start.12 = (bf16[96,1024]{1,0:T(8,128)(2,1)}, bf16[96,1024]{1,0:T(8,128)(2,1)S(1)}, u32[]{:S(2)}, u32[]{:S(2)}) collective-permute-start(bf16[96,1024]{1,0:T(8,128)(2,1)} %copy-done.6), channel_id=1, source_target_pairs={{0,960},{32,992},{64,0},{96,32},{128,64},{160,96},{192,128},{224,1... | collective-permute-start | bytes 589832 | tf_op jit(solution)/shard_map/ppermute | solution.py:227
  93.0 17.3 %collective-permute-start.15 = (bf16[96,1024]{1,0:T(8,128)(2,1)}, bf16[96,1024]{1,0:T(8,128)(2,1)S(1)}, u32[]{:S(2)}, u32[]{:S(2)}) collective-permute-start(bf16[96,1024]{1,0:T(8,128)(2,1)} %collective-permute-done.11.refs_3_), channel_id=1, source_target_pairs={{0,64},{32,96},{64,128},{96,160},{128,192},{160,224},{192,256},{22... | collective-permute-start | bytes 589832 | tf_op jit(solution)/shard_map/ppermute | solution.py:226
  94.9 18.0 %collective-permute-start.24 = (bf16[96,1024]{1,0:T(8,128)(2,1)S(1)}, bf16[96,1024]{1,0:T(8,128)(2,1)}, u32[]{:S(2)}, u32[]{:S(2)}) collective-permute-start(bf16[96,1024]{1,0:T(8,128)(2,1)S(1)} %collective-permute-done.8.refs_7_), channel_id=1, source_target_pairs={{0,960},{32,992},{64,0},{96,32},{128,64},{160,96},{192,128},{224,1... | collective-permute-start | bytes 589832 | tf_op jit(solution)/shard_map/ppermute | solution.py:206
  101.0 18.0 %collective-permute-start.23 = (bf16[96,1024]{1,0:T(8,128)(2,1)S(1)}, bf16[96,1024]{1,0:T(8,128)(2,1)}, u32[]{:S(2)}, u32[]{:S(2)}) collective-permute-start(bf16[96,1024]{1,0:T(8,128)(2,1)S(1)} %collective-permute-done.22.refs_2_), channel_id=1, source_target_pairs={{0,64},{32,96},{64,128},{96,160},{128,192},{160,224},{192,256},{22... | collective-permute-start | bytes 589832 | tf_op jit(solution)/shard_map/ppermute | solution.py:204
  102.9 0.7 copy-start.4
  103.6 17.3 %collective-permute-start.13 = (bf16[96,1024]{1,0:T(8,128)(2,1)S(1)}, bf16[96,1024]{1,0:T(8,128)(2,1)}, u32[]{:S(2)}, u32[]{:S(2)}) collective-permute-start(bf16[96,1024]{1,0:T(8,128)(2,1)S(1)} %collective-permute-done.12.refs_8_), channel_id=1, source_target_pairs={{0,960},{32,992},{64,0},{96,32},{128,64},{160,96},{192,128},{224,1... | collective-permute-start | bytes 589832 | tf_op jit(solution)/shard_map/ppermute | solution.py:227
  109.6 0.7 copy-start.8
  110.3 16.6 %collective-permute-start.16 = (bf16[96,1024]{1,0:T(8,128)(2,1)S(1)}, bf16[96,1024]{1,0:T(8,128)(2,1)}, u32[]{:S(2)}, u32[]{:S(2)}) collective-permute-start(bf16[96,1024]{1,0:T(8,128)(2,1)S(1)} %collective-permute-done.15.refs_2_), channel_id=1, source_target_pairs={{0,64},{32,96},{64,128},{96,160},{128,192},{160,224},{192,256},{22... | collective-permute-start | bytes 589832 | tf_op jit(solution)/shard_map/ppermute | solution.py:226
  112.3 0.7 copy-start.10
  112.9 16.1 %collective-permute-start.25 = (bf16[96,1024]{1,0:T(8,128)(2,1)}, bf16[96,1024]{1,0:T(8,128)(2,1)}, u32[]{:S(2)}, u32[]{:S(2)}) collective-permute-start(bf16[96,1024]{1,0:T(8,128)(2,1)} %collective-permute-done.24.refs_8_), channel_id=1, source_target_pairs={{0,960},{32,992},{64,0},{96,32},{128,64},{160,96},{192,128},{224,1... | collective-permute-start | bytes 589832 | tf_op jit(solution)/shard_map/ppermute | solution.py:206
  119.0 18.0 %collective-permute-start.29 = (bf16[96,1024]{1,0:T(8,128)(2,1)}, bf16[96,1024]{1,0:T(8,128)(2,1)}, u32[]{:S(2)}, u32[]{:S(2)}) collective-permute-start(bf16[96,1024]{1,0:T(8,128)(2,1)} %collective-permute-done.23.refs_1_), channel_id=1, source_target_pairs={{0,64},{32,96},{64,128},{96,160},{128,192},{160,224},{192,256},{22... | collective-permute-start | bytes 589832 | tf_op jit(solution)/shard_map/ppermute | solution.py:204
  120.9 18.6 %collective-permute-start.14 = (bf16[96,1024]{1,0:T(8,128)(2,1)}, bf16[96,1024]{1,0:T(8,128)(2,1)}, u32[]{:S(2)}, u32[]{:S(2)}) collective-permute-start(bf16[96,1024]{1,0:T(8,128)(2,1)} %collective-permute-done.13.refs_2_), channel_id=1, source_target_pairs={{0,960},{32,992},{64,0},{96,32},{128,64},{160,96},{192,128},{224,1... | collective-permute-start | bytes 589832 | tf_op jit(solution)/shard_map/ppermute | solution.py:227
  127.0 18.6 %collective-permute-start.17 = (bf16[96,1024]{1,0:T(8,128)(2,1)}, bf16[96,1024]{1,0:T(8,128)(2,1)}, u32[]{:S(2)}, u32[]{:S(2)}) collective-permute-start(bf16[96,1024]{1,0:T(8,128)(2,1)} %collective-permute-done.16.refs_1_), channel_id=1, source_target_pairs={{0,64},{32,96},{64,128},{96,160},{128,192},{160,224},{192,256},{22... | collective-permute-start | bytes 589832 | tf_op jit(solution)/shard_map/ppermute | solution.py:226
  129.0 28.9 %collective-permute-start.26 = (bf16[96,1024]{1,0:T(8,128)(2,1)}, bf16[96,1024]{1,0:T(8,128)(2,1)}, u32[]{:S(2)}, u32[]{:S(2)}) collective-permute-start(bf16[96,1024]{1,0:T(8,128)(2,1)} %collective-permute-done.25.refs_2_), channel_id=1, source_target_pairs={{0,960},{32,992},{64,0},{96,32},{128,64},{160,96},{192,128},{224,1... | collective-permute-start | bytes 589832 | tf_op jit(solution)/shard_map/ppermute | solution.py:206
  137.0 24.6 %collective-permute-start.30 = (bf16[96,1024]{1,0:T(8,128)(2,1)}, bf16[96,1024]{1,0:T(8,128)(2,1)}, u32[]{:S(2)}, u32[]{:S(2)}) collective-permute-start(bf16[96,1024]{1,0:T(8,128)(2,1)} %collective-permute-done.29.refs_9_), channel_id=1, source_target_pairs={{0,64},{32,96},{64,128},{96,160},{128,192},{160,224},{192,256},{22... | collective-permute-start | bytes 589832 | tf_op jit(solution)/shard_map/ppermute | solution.py:204
  145.5 23.3 %copy-start.1 = (bf16[96,1024]{1,0:T(8,128)(2,1)S(1)}, bf16[96,1024]{1,0:T(8,128)(2,1)}, u32[]{:S(2)}) copy-start(bf16[96,1024]{1,0:T(8,128)(2,1)} %copy-done) | copy-start | bytes 589828
  145.5 23.3 %copy-start.3 = (bf16[96,1024]{1,0:T(8,128)(2,1)S(1)}, bf16[96,1024]{1,0:T(8,128)(2,1)}, u32[]{:S(2)}) copy-start(bf16[96,1024]{1,0:T(8,128)(2,1)} %copy-done.2) | copy-start | bytes 589828
  145.5 23.4 %copy-start.7 = (bf16[96,1024]{1,0:T(8,128)(2,1)S(1)}, bf16[96,1024]{1,0:T(8,128)(2,1)}, u32[]{:S(2)}) copy-start(bf16[96,1024]{1,0:T(8,128)(2,1)} %copy-done.6) | copy-start | bytes 589828
  145.5 23.4 %copy-start.9 = (bf16[96,1024]{1,0:T(8,128)(2,1)S(1)}, bf16[96,1024]{1,0:T(8,128)(2,1)}, u32[]{:S(2)}) copy-start(bf16[96,1024]{1,0:T(8,128)(2,1)} %copy-done.8) | copy-start | bytes 589828
  145.6 23.4 %copy-start.11 = (bf16[96,1024]{1,0:T(8,128)(2,1)S(1)}, bf16[96,1024]{1,0:T(8,128)(2,1)}, u32[]{:S(2)}) copy-start(bf16[96,1024]{1,0:T(8,128)(2,1)} %copy-done.10) | copy-start | bytes 589828
  151.1 17.7 %collective-permute-start.18 = (bf16[96,1024]{1,0:T(8,128)(2,1)}, bf16[96,1024]{1,0:T(8,128)(2,1)S(1)}, u32[]{:S(2)}, u32[]{:S(2)}) collective-permute-start(bf16[96,1024]{1,0:T(8,128)(2,1)} %collective-permute-done.14.refs_3_), channel_id=1, source_target_pairs={{0,960},{32,992},{64,0},{96,32},{128,64},{160,96},{192,128},{224,1... | collective-permute-start | bytes 589832 | tf_op jit(solution)/shard_map/ppermute | solution.py:227
  153.6 15.2 %collective-permute-start.19 = (bf16[96,1024]{1,0:T(8,128)(2,1)}, bf16[96,1024]{1,0:T(8,128)(2,1)S(1)}, u32[]{:S(2)}, u32[]{:S(2)}) collective-permute-start(bf16[96,1024]{1,0:T(8,128)(2,1)} %collective-permute-done.17.refs_9_), channel_id=1, source_target_pairs={{0,64},{32,96},{64,128},{96,160},{128,192},{160,224},{192,256},{22... | collective-permute-start | bytes 589832 | tf_op jit(solution)/shard_map/ppermute | solution.py:226
  157.9 19.7 %collective-permute-start.27 = (bf16[96,1024]{1,0:T(8,128)(2,1)}, bf16[96,1024]{1,0:T(8,128)(2,1)S(1)}, u32[]{:S(2)}, u32[]{:S(2)}) collective-permute-start(bf16[96,1024]{1,0:T(8,128)(2,1)} %collective-permute-done.26.refs_3_), channel_id=1, source_target_pairs={{0,960},{32,992},{64,0},{96,32},{128,64},{160,96},{192,128},{224,1... | collective-permute-start | bytes 589832 | tf_op jit(solution)/shard_map/ppermute | solution.py:206
  161.6 19.2 %collective-permute-start.31 = (bf16[96,1024]{1,0:T(8,128)(2,1)}, bf16[96,1024]{1,0:T(8,128)(2,1)S(1)}, u32[]{:S(2)}, u32[]{:S(2)}) collective-permute-start(bf16[96,1024]{1,0:T(8,128)(2,1)} %collective-permute-done.30.refs_8_), channel_id=1, source_target_pairs={{0,64},{32,96},{64,128},{96,160},{128,192},{160,224},{192,256},{22... | collective-permute-start | bytes 589832 | tf_op jit(solution)/shard_map/ppermute | solution.py:204
  170.7 18.3 %copy-start.5 = (bf16[96,1024]{1,0:T(8,128)(2,1)S(1)}, bf16[96,1024]{1,0:T(8,128)(2,1)}, u32[]{:S(2)}) copy-start(bf16[96,1024]{1,0:T(8,128)(2,1)} %copy-done.4) | copy-start | bytes 589828
  170.7 13.7 %collective-permute-start.20 = (bf16[96,1024]{1,0:T(8,128)(2,1)S(1)}, bf16[96,1024]{1,0:T(8,128)(2,1)S(1)}, u32[]{:S(2)}, u32[]{:S(2)}) collective-permute-start(bf16[96,1024]{1,0:T(8,128)(2,1)S(1)} %collective-permute-done.18.refs_4_), channel_id=1, source_target_pairs={{0,960},{32,992},{64,0},{96,32},{128,64},{160,96},{192,128},{224,1... | collective-permute-start | bytes 589832 | tf_op jit(solution)/shard_map/ppermute | solution.py:227
  172.8 16.1 %collective-permute-start.21 = (bf16[96,1024]{1,0:T(8,128)(2,1)S(1)}, bf16[96,1024]{1,0:T(8,128)(2,1)S(1)}, u32[]{:S(2)}, u32[]{:S(2)}) collective-permute-start(bf16[96,1024]{1,0:T(8,128)(2,1)S(1)} %collective-permute-done.19.refs_8_), channel_id=1, source_target_pairs={{0,64},{32,96},{64,128},{96,160},{128,192},{160,224},{192,256},{22... | collective-permute-start | bytes 589832 | tf_op jit(solution)/shard_map/ppermute | solution.py:226
  177.6 13.2 %collective-permute-start.28 = (bf16[96,1024]{1,0:T(8,128)(2,1)S(1)}, bf16[96,1024]{1,0:T(8,128)(2,1)S(1)}, u32[]{:S(2)}, u32[]{:S(2)}) collective-permute-start(bf16[96,1024]{1,0:T(8,128)(2,1)S(1)} %collective-permute-done.27.refs_4_), channel_id=1, source_target_pairs={{0,960},{32,992},{64,0},{96,32},{128,64},{160,96},{192,128},{224,1... | collective-permute-start | bytes 589832 | tf_op jit(solution)/shard_map/ppermute | solution.py:206
  180.8 14.2 %collective-permute-start.32 = (bf16[96,1024]{1,0:T(8,128)(2,1)S(1)}, bf16[96,1024]{1,0:T(8,128)(2,1)S(1)}, u32[]{:S(2)}, u32[]{:S(2)}) collective-permute-start(bf16[96,1024]{1,0:T(8,128)(2,1)S(1)} %collective-permute-done.31.refs_7_), channel_id=1, source_target_pairs={{0,64},{32,96},{64,128},{96,160},{128,192},{160,224},{192,256},{22... | collective-permute-start | bytes 589832 | tf_op jit(solution)/shard_map/ppermute | solution.py:204
  197.1 26.2 %collective-permute-start.33 = (bf16[192,1024]{1,0:T(8,128)(2,1)S(1)}, bf16[192,1024]{1,0:T(8,128)(2,1)S(1)}, u32[]{:S(2)}, u32[]{:S(2)}) collective-permute-start(bf16[192,1024]{1,0:T(8,128)(2,1)S(1)} %get-tuple-element.51), channel_id=1, source_target_pairs={{0,32},{32,0},{64,96},{96,64},{128,160},{160,128},{192,224},{224,1... | collective-permute-start | bytes 1179656 | tf_op jit(solution)/shard_map/ppermute | solution.py:233
  200.2 8.7 %collective-permute-start.34 = (bf16[96,1024]{1,0:T(8,128)(2,1)S(1)}, bf16[96,1024]{1,0:T(8,128)(2,1)S(1)}, u32[]{:S(2)}, u32[]{:S(2)}) collective-permute-start(bf16[96,1024]{1,0:T(8,128)(2,1)S(1)} %collective-permute-done.20.refs_5_), channel_id=1, source_target_pairs={{0,960},{32,992},{64,0},{96,32},{128,64},{160,96},{192,128},{224,1... | collective-permute-start | bytes 589832 | tf_op jit(solution)/shard_map/ppermute | solution.py:227
  210.8 18.7 %collective-permute-start.35 = (bf16[192,1024]{1,0:T(8,128)(2,1)S(1)}, bf16[192,1024]{1,0:T(8,128)(2,1)S(1)}, u32[]{:S(2)}, u32[]{:S(2)}) collective-permute-start(bf16[192,1024]{1,0:T(8,128)(2,1)S(1)} %get-tuple-element.55), channel_id=1, source_target_pairs={{0,992},{32,64},{64,32},{96,128},{128,96},{160,192},{192,160},{224... | collective-permute-start | bytes 1179656 | tf_op jit(solution)/shard_map/ppermute | solution.py:234

commit v2 on v0

--- a/solution.py
+++ b/solution.py
@@ -1,6 +1,8 @@
 import jax
 import jax.numpy as jnp
 from jax import lax
+from jax.experimental import pallas as pl
+from jax.experimental.pallas import tpu as pltpu
 from jax.sharding import PartitionSpec as P
 
 TOP = 2
@@ -21,6 +23,34 @@
 
 def add_counts(earlier, later):
     return earlier + later
+
+
+def product_kernel(left_ref, right_ref, out_ref):
+    out_ref[...] = jnp.dot(
+        left_ref[...], right_ref[...], preferred_element_type=jnp.float32
+    ).astype(out_ref.dtype)
+
+
+def product(left, right):
+    rows, depth = left.shape
+    columns = right.shape[1]
+    width = 512
+    return pl.pallas_call(
+        product_kernel,
+        out_shape=jax.ShapeDtypeStruct((rows, columns), jnp.bfloat16),
+        grid=(columns // width,),
+        in_specs=[
+            pl.BlockSpec((rows, depth), lambda i: (0, 0)),
+            pl.BlockSpec((depth, width), lambda i: (0, i)),
+        ],
+        out_specs=pl.BlockSpec((rows, width), lambda i: (0, i)),
+        compiler_params=pltpu.CompilerParams(vmem_limit_bytes=16 << 20),
+        cost_estimate=pl.CostEstimate(
+            flops=2 * rows * depth * columns,
+            bytes_accessed=2 * (rows * depth + depth * columns + rows * columns),
+            transcendentals=0,
+        ),
+    )(left, right)
 
 
 def body(out_grad, expert_ids, combine, hidden):
@@ -55,13 +85,8 @@
     arranged = arranged.at[arrived_slots.reshape(-1)].set(arrived_rows.reshape(-1, features))[
         :capacity
     ]
-    gradient_sum = lax.dot_general(
-        lax.all_gather(hidden[0], "dp", axis=0, tiled=True),
-        arranged,
-        (((0,), (0,)), ((), ())),
-        preferred_element_type=jnp.float32,
-    )
-    return gradient_sum.astype(jnp.bfloat16)[None]
+    gathered = lax.all_gather(hidden[0], "dp", axis=0, tiled=True)
+    return product(arranged.T, gathered).T[None]
 
 
 def solution(mesh):

time: 202 us -> 204 us (level)
  matrix products: 8.38 us -> 0 us
  Pallas kernels: 0 us -> 5.74 us
  local copies, waits for them, and re-layouts: 19.1 us -> 23.8 us
    dot_general x1 -> x0, matrix products: 8.38 us -> none  [body(): lax.dot_general(lax.all_gather(hidden[0], 'dp', axis=0, tiled=True), arra...]
    pallas_call x0 -> x1, Pallas kernels: none -> 5.74 us  [product(): pl.pallas_call(product_kernel, out_shape=jax.ShapeDtypeStruct((rows, colu...]
    unnamed x5 -> x8, local copies, waits for them, and re-layouts: 3.24 us -> 8.07 us
where the time goes in v2:
time: 204 us; the launch traced here: 203 us
  waiting for transfers between devices  132 us (65%)
  local copies, waits for them, and re-layouts  23.8 us (12%)
  between operations  14.2 us (7%)
  other arithmetic  9.93 us (5%)
  blocking collectives  9.22 us (5%)
  starting transfers between devices  8.04 us (4%)
  Pallas kernels  5.74 us (3%)
    all_gather x1, waiting for transfers between devices, body(): gathered = lax.all_gather(hidden[0], 'dp', axis=0, tiled=True)  118 us
    all_to_all x1, waiting for transfers between devices, body(): lax.all_to_all(send_rows, 'expert', split_axis=0, concat_axis=0, tiled=True)  13 us
    unnamed x1, blocking collectives  9.22 us
    unnamed x8, local copies, waits for them, and re-layouts  8.07 us
    scatter x1, local copies, waits for them, and re-layouts, body(): arranged.at[arrived_slots.reshape(-1)]  7.29 us
    scatter x1, other arithmetic, body(): jnp.zeros((experts * block_most, features), jnp.bfloat16).at[send_index]  6.33 us
    pallas_call x1, Pallas kernels, product(): pl.pallas_call(product_kernel, out_shape=jax.ShapeDtypeStruct((rows, colu...  5.74 us
    all_to_all x1, starting transfers between devices, body(): lax.all_to_all(send_rows, 'expert', split_axis=0, concat_axis=0, tiled=True)  4.72 us
  transfers between devices with their start and end apart: 3, of which 2 were waited for; matrix products, arithmetic and copies ran while one was open for 14% of the time, Pallas kernels for 0%

profile of v2, /device:TPU:24, one launch (start us, length us, event | category | flops | bytes accessed | tf_op | source)
XLA Modules:
  0.0 203.1 jit_solution(17004530819565687039)
XLA Ops:
  6.5 0.0 all-gather.4.cloned.1.call-start
  6.5 0.7 all-gather.4.cloned.1.call-update
  7.3 0.8 copy.6
  8.1 0.2 eq.25
  8.3 0.2 eq.29
  8.5 0.7 broadcast_multiply_fusion
  9.1 0.1 copy.5
  9.3 0.2 mul.47
  9.5 1.3 dynamic-slice
  11.5 0.1 convert_reduce_fusion
  11.6 0.2 dynamic-update-slice
  11.9 9.2 %all-reduce = s32[64]{0:T(128)S(1)} all-reduce(s32[64]{0:T(128)S(1)} %dynamic-update-slice), channel_id=2, replica_groups=mesh['dp'=32,'expert'=8,'tensor'=4] {'expert'}, use_global_device_ids=true, to_apply=%add | all-reduce | flops 64 | bytes 512
  21.1 0.1 reshape.124
  21.2 2.3 %reduce-window.6 = s32[8,8,128]{2,1,0:T(8,128)S(1)} reduce-window(s32[8,8,128]{2,1,0:T(8,128)S(1)} %fusion.7, s32[]{:T(128)} %constant.44.clone.1), window={size=1x1x128 pad=0_0x0_0x127_0}, to_apply=%region_0.0 | reduce-window | flops 1040384 | bytes 65540 | tf_op jit(solution)/shard_map/reduce-window
  23.5 0.3 slice_reduce_fusion
  23.7 0.2 reduce-window.9
  23.9 0.1 add_bitcast_fusion
  24.0 0.3 while.14
  24.3 0.1 select_reduce_fusion
  24.4 4.3 %scatter_custom_fusion = s32[1536]{0:T(1024)S(1)} fusion(s32[1024]{0:T(1024)S(1)} %bitcast.33, s32[1024]{0:T(1024)S(1)} %add.67, s32[]{:T(128)} %constant.42.clone.1), kind=kCustom, calls=%fused_computation.25 | custom fusion | bytes 6148 | tf_op jit(solution)/shard_map/scatter | solution.py:76
  28.7 0.7 all_to_all.9
  29.4 3.3 %all-to-all-start = ((s32[8,1,192]{2,1,0:T(1,128)}), s32[8,1,192]{2,1,0:T(1,128)S(1)}, u32[]{:S(2)}, u32[]{:S(2)}) async-start(s32[8,1,192]{2,1,0:T(1,128)} %all_to_all.9), calls=%async_computation | async-start | bytes 16384 | tf_op jit(solution)/shard_map/all_to_all | solution.py:82
  32.7 0.8 copy.8
  33.6 0.2 mul.51
  33.7 1.1 copy.9
  34.8 0.4 mul.53
  35.2 0.7 mul.54
  35.9 6.3 %scatter_custom_fusion.1 = bf16[1536,192]{1,0:T(8,128)(2,1)} fusion(s32[1024]{0:T(1024)S(1)} %bitcast.34, f32[1024,192]{1,0:T(8,128)S(1)} %mul.54, f32[1024]{0:T(1024)S(1)} %mul.51, bf16[]{:T(256)} %constant.41.clone.1), kind=kCustom, calls=%fused_computation.6 | custom fusion | flops 393216 | bytes 1642498 | tf_op jit(solution)/shard_map/scatter | solution.py:74
  42.2 0.0 all-to-all-done
  42.2 4.7 %all-to-all-start.1 = ((bf16[8,192,192]{2,1,0:T(8,128)(2,1)}), bf16[8,192,192]{2,1,0:T(8,128)(2,1)S(1)}, u32[]{:S(2)}, u32[]{:S(2)}) async-start(bf16[8,192,192]{2,1,0:T(8,128)(2,1)} %bitcast.4), calls=%async_computation.1 | async-start | bytes 1572864 | tf_op jit(solution)/shard_map/all_to_all | solution.py:81
  47.0 0.1 reshape.97
  47.1 13.0 %all-to-all-done.1 = bf16[8,192,192]{2,1,0:T(8,128)(2,1)S(1)} async-done(((bf16[8,192,192]{2,1,0:T(8,128)(2,1)}), bf16[8,192,192]{2,1,0:T(8,128)(2,1)S(1)}, u32[]{:S(2)}, u32[]{:S(2)}) %all-to-all-start.1) | async-done | bytes 589856 | tf_op jit(solution)/shard_map/all_to_all | solution.py:81
  60.1 7.3 %scatter_custom_fusion.2 = bf16[1537,192]{1,0:T(8,128)(2,1)S(1)} fusion(s32[1536]{0:T(1024)S(1)} %fusion.8, bf16[1536,192]{1,0:T(8,128)(2,1)S(1)} %bitcast.30, bf16[]{:T(256)} %constant.41.clone.1), kind=kCustom, calls=%fused_computation.8 | custom fusion | bytes 590210 | tf_op jit(solution)/shard_map/scatter | solution.py:85
  67.4 0.1 slice.13
  67.5 0.3 copy.11
  67.7 118.2 %all-gather.4.cloned.1.call-done = bf16[1,1536,4096]{2,1,0:T(8,128)(2,1)} async-done(((bf16[1,48,4096]{2,1,0:T(8,128)(2,1)}), bf16[1,1536,4096]{2,1,0:T(8,128)(2,1)}) %all-gather.4.cloned.1.call-update) | async-done | bytes 12582928 | tf_op jit(solution)/shard_map/all_gather | solution.py:88
  185.9 0.0 copy-start
  186.0 4.6 %copy-done = bf16[1,1536,4096]{2,1,0:T(8,128)(2,1)S(1)} copy-done((bf16[1,1536,4096]{2,1,0:T(8,128)(2,1)S(1)}, bf16[1,1536,4096]{2,1,0:T(8,128)(2,1)}, u32[]{:S(2)}) %copy-start) | copy-done | bytes 12582936
  190.5 5.7 %shard_map.46 = bf16[192,4096]{1,0:T(8,128)(2,1)} custom-call(bf16[192,1536]{1,0:T(8,128)(2,1)S(1)} %bitcast.29, bf16[1536,4096]{1,0:T(8,128)(2,1)S(1)} %bitcast.28), custom_call_target="tpu_custom_call" | custom-call | flops 2415919104 | bytes 14745600 | tf_op jit(solution)/shard_map/pallas_call | solution.py:38
  (15 shorter events, 0.2 us)
Async XLA Ops:
  6.5 179.4 %all-gather.4.cloned.1.call-start = ((), (), s32[]{:S(2)}) async-start(), calls=%async_computation.2 | async-start | bytes 12976128 | tf_op jit(solution)/shard_map/all_gather | solution.py:88
  29.4 12.8 %all-to-all-start = ((s32[8,1,192]{2,1,0:T(1,128)}), s32[8,1,192]{2,1,0:T(1,128)S(1)}, u32[]{:S(2)}, u32[]{:S(2)}) async-start(s32[8,1,192]{2,1,0:T(1,128)} %all_to_all.9), calls=%async_computation | async-start | bytes 16384 | tf_op jit(solution)/shard_map/all_to_all | solution.py:82
  42.2 17.9 %all-to-all-start.1 = ((bf16[8,192,192]{2,1,0:T(8,128)(2,1)}), bf16[8,192,192]{2,1,0:T(8,128)(2,1)S(1)}, u32[]{:S(2)}, u32[]{:S(2)}) async-start(bf16[8,192,192]{2,1,0:T(8,128)(2,1)} %bitcast.4), calls=%async_computation.1 | async-start | bytes 1572864 | tf_op jit(solution)/shard_map/all_to_all | solution.py:81
  185.9 4.6 %copy-start = (bf16[1,1536,4096]{2,1,0:T(8,128)(2,1)S(1)}, bf16[1,1536,4096]{2,1,0:T(8,128)(2,1)}, u32[]{:S(2)}) copy-start(bf16[1,1536,4096]{2,1,0:T(8,128)(2,1)} %all-gather.4.cloned.1.call-done) | copy-start | bytes 37748740
Sparse Core Ops, SparseCore 0:
  10.0 175.8 all-gather.3

commit v3 on v1

--- a/solution.py
+++ b/solution.py
@@ -7,6 +7,7 @@
 
 LANES = 256
 PAIRS = 16
+CUT = 1280
 COUNT = 192
 
 
@@ -14,7 +15,7 @@
     return lax.dot_general(a, b, (((da,), (db,)), ((), ())), preferred_element_type=jnp.float32)
 
 
-def send_kernel(ids_ref, weights_ref, first_ref, own_ref, second_ref, out_ref):
+def send_kernel(ids_ref, weights_ref, own_ref, partner_ref, out_ref):
     features, tokens = own_ref.shape
     experts = out_ref.shape[0]
     ids, weights = ids_ref[...], weights_ref[...]
@@ -34,7 +35,7 @@
         count = jnp.sum(jnp.where(ranks[:, e : e + 1] >= 0, 1.0, 0.0), axis=0, keepdims=True)
         pick = jnp.where(chosen, 1.0, 0.0).astype(jnp.bfloat16)
         at_count = lax.broadcasted_iota(jnp.int32, (features, LANES), 1) == COUNT
-        for part, ref in enumerate((first_ref, own_ref, second_ref)):
+        for part, ref in enumerate((own_ref, partner_ref)):
             rows = dot(ref[...], pick) * scale
             out_ref[e, part * features : (part + 1) * features, :] = jnp.where(
                 at_count, count, rows
@@ -99,35 +100,30 @@
     return pl.CostEstimate(flops=flops, bytes_accessed=bytes_accessed, transcendentals=0)
 
 
-def scaled_rows(out_grad, expert_ids, combine, grad_a, grad_b, experts):
-    features, tokens = out_grad.shape
-    wide = 3 * features
+def scaled_rows(own, expert_ids, combine, partner, experts):
+    features, tokens = own.shape
+    wide = 2 * features
     return pl.pallas_call(
         send_kernel,
         out_shape=jax.ShapeDtypeStruct((experts, wide, LANES), jnp.bfloat16),
         compiler_params=params(12),
         cost_estimate=cost(2 * experts * LANES * tokens * wide, 6 << 20),
-    )(expert_ids, combine, grad_a, out_grad, grad_b)
-
-
-def place(rows, even, z, share, near, features, capacity):
+    )(expert_ids, combine, own, partner)
+
+
+def place(rows, bases, capacity):
     experts, wide, _ = rows.shape
-    base_a = share * (jnp.where(even, z, z - 1) - 2 * near)
-    base_b = share * (jnp.where(even, z - 1, z) - 2 * near)
-    bases = jnp.stack([base_a % capacity, base_b % capacity]).astype(jnp.int32)
+    table = jax.ShapeDtypeStruct((wide, capacity), jnp.bfloat16)
     return pl.pallas_call(
         place_kernel,
-        out_shape=[jax.ShapeDtypeStruct((2 * features, capacity), jnp.bfloat16)] * 2,
+        out_shape=[table, table],
         in_specs=[
             pl.BlockSpec(memory_space=pltpu.SMEM),
             pl.BlockSpec(memory_space=pltpu.VMEM),
         ],
-        scratch_shapes=[
-            pltpu.VMEM((2 * features, capacity + 384), jnp.float32),
-            pltpu.VMEM((2 * features, capacity + 384), jnp.float32),
-        ],
+        scratch_shapes=[pltpu.VMEM((wide, capacity + 384), jnp.float32)] * 2,
         compiler_params=params(16),
-        cost_estimate=cost(8 * features * experts * LANES * 384, 6 << 20),
+        cost_estimate=cost(4 * wide * experts * LANES * 384, 6 << 20),
     )(bases, rows)
 
 
@@ -177,70 +173,57 @@
     hidden = hidden[0]
     share, units = hidden.shape
     capacity = share * planes
-    quarter = units // 4
+    half = units // 2
     z = lax.axis_index("dp")
     even = z % 2 == 0
 
-    swap_a = [(i, i ^ 1) for i in range(planes)]
-    swap_b = [(i, ((i + 1) ^ 1) - 1) for i in range(planes)]
-    swap_b = [(i, j % planes) for i, j in swap_b]
+    swap = [(i, i ^ 1) for i in range(planes)]
     right = [(i, (i + 2) % planes) for i in range(planes)]
     left = [(i, (i - 2) % planes) for i in range(planes)]
-
-    q = [hidden[:, i * quarter : (i + 1) * quarter] for i in range(4)]
-    keep_a, give_a = jnp.where(even, q[0], q[1]), jnp.where(even, q[1], q[0])
-    keep_b, give_b = jnp.where(even, q[3], q[2]), jnp.where(even, q[2], q[3])
-    got_a = lax.ppermute(give_a, "dp", swap_a)
-    got_b = lax.ppermute(give_b, "dp", swap_b)
-    grad_a = lax.ppermute(out_grad, "dp", swap_a)
-    grad_b = lax.ppermute(out_grad, "dp", swap_b)
-    block_a = jnp.concatenate([jnp.where(even, keep_a, got_a), jnp.where(even, got_a, keep_a)])
-    block_b = jnp.concatenate([jnp.where(even, got_b, keep_b), jnp.where(even, keep_b, got_b)])
-
-    chain_a, chain_b = {0: block_a}, {0: block_b}
-    half = PAIRS // 2
-    near = half // 2
-    for s in range(1, half + 1):
-        chain_a[PAIRS - s] = lax.ppermute(chain_a[(1 - s) % PAIRS], "dp", right)
-        if s < half:
-            chain_a[s] = lax.ppermute(chain_a[s - 1], "dp", left)
+    keep = jnp.where(even, hidden[:, :half], hidden[:, half:])
+    give = jnp.where(even, hidden[:, half:], hidden[:, :half])
+
+    got = lax.ppermute(give, "dp", swap)
+    block = jnp.concatenate([jnp.where(even, keep, got), jnp.where(even, got, keep)])
+
+    parity = [list(range(r, planes, 2)) for r in range(2)]
+    gathered = lax.all_gather(
+        block[:, :CUT], "dp", axis=0, tiled=True, axis_index_groups=parity
+    )
+
+    chain = {0: block[:, CUT:]}
+    steps = PAIRS // 2
+    near = steps // 2
+    for s in range(1, steps + 1):
         if s == 2:
-            ids = after(after(expert_ids, chain_a, 1), chain_b, 1)
-            rows = scaled_rows(out_grad, ids, combine, grad_a, grad_b, experts)
-            (rows,) = before([rows], chain_b, 1)
+            out_grad = after(out_grad, chain, 1)
+            partner = lax.ppermute(out_grad, "dp", swap)
         if s == 3:
-            rows = after(after(rows, chain_a, 2), chain_b, 2)
+            ids = after(expert_ids, chain, 2)
+            rows = scaled_rows(out_grad, ids, combine, partner, experts)
+        if s == 4:
+            rows = after(rows, chain, 3)
             rows = lax.all_to_all(rows, "expert", split_axis=0, concat_axis=0, tiled=True)
         if s == 6:
-            rows = after(rows, chain_b, 5)
-            arranged = place(rows, even, z, share, near, features, capacity)
-            arranged = before(arranged, chain_b, 5)
+            base = share * (jnp.where(even, z, z - 1) - 2 * near)
+            bases = jnp.stack([jnp.int32(0), base % capacity]).astype(jnp.int32)
+            plain, turned = place(after(rows, chain, 5), bases, capacity)
+            plain, turned = before([plain, turned], chain, 5)
         if s == 7:
-            total_b = near_product(chain_b, after(arranged[1], chain_b, 6), near)
-            (total_b,) = before([total_b], chain_b, 6)
-        if s == 8:
-            total_a = near_product(chain_a, after(arranged[0], chain_b, 7), near)
-            (total_a,) = before([total_a], chain_b, 7)
-            totals = total_a, total_b
-        if s < half:
-            chain_b[PAIRS - s] = lax.ppermute(chain_b[(1 - s) % PAIRS], "dp", right)
-        chain_b[s] = lax.ppermute(chain_b[s - 1], "dp", left)
-
-    results = [
-        far_product(t, c, a, near) for t, c, a in zip(totals, (chain_a, chain_b), arranged)
-    ]
-    (theirs_a, mine_a), (mine_b, theirs_b) = results
-    back_a = lax.ppermute(theirs_a, "dp", swap_a)
-    back_b = lax.ppermute(theirs_b, "dp", swap_b)
-    out = jnp.concatenate(
-        [
-            jnp.where(even, mine_a, back_a),
-            jnp.where(even, back_a, mine_a),
-            jnp.where(even, back_b, mine_b),
-            jnp.where(even, mine_b, back_b),
-        ],
-        axis=1,
-    )
+            total = near_product(chain, after(turned, chain, 6), near)
+            (total,) = before([total], chain, 6)
+        chain[PAIRS - s] = lax.ppermute(chain[(1 - s) % PAIRS], "dp", right)
+        if s < steps:
+            chain[s] = lax.ppermute(chain[s - 1], "dp", left)
+    mine_last, theirs_last = far_product(total, chain, turned, near)
+    back_last = lax.ppermute(theirs_last, "dp", swap)
+
+    gathered = lax.optimization_barrier((gathered, chain[steps]))[0]
+    first = dot(plain, gathered).astype(jnp.bfloat16)
+    back_first = lax.ppermute(first[features:], "dp", swap)
+    mine = jnp.concatenate([first[:features], mine_last], axis=1)
+    back = jnp.concatenate([back_first, back_last], axis=1)
+    out = jnp.concatenate([jnp.where(even, mine, back), jnp.where(even, back, mine)], axis=1)
     return out.T[None]
 
 

time: 234 us -> 235 us (level)
  the two profiles are of different devices: /device:TPU:24 before, /device:TPU:32 now
where the time goes in v3:
time: 235 us; the launch traced here: 234 us
  waiting for transfers between devices  104 us (44%)
  starting transfers between devices  90.8 us (39%)
  between operations  13.8 us (6%)
  Pallas kernels  10.3 us (4%)
  local copies, waits for them, and re-layouts  5.96 us (3%)
  other arithmetic  4.56 us (2%)
  matrix products  4.16 us (2%)
    ppermute x8, waiting for transfers between devices, body(): chain[PAIRS - s] = lax.ppermute(chain[(1 - s) % PAIRS], 'dp', right)  44.1 us
    ppermute x7, starting transfers between devices, body(): chain[s] = lax.ppermute(chain[s - 1], 'dp', left)  42 us
    ppermute x7, waiting for transfers between devices, body(): chain[s] = lax.ppermute(chain[s - 1], 'dp', left)  28.1 us
    ppermute x1, waiting for transfers between devices, body(): partner = lax.ppermute(out_grad, 'dp', swap)  21.9 us
    ppermute x8, starting transfers between devices, body(): chain[PAIRS - s] = lax.ppermute(chain[(1 - s) % PAIRS], 'dp', right)  16.5 us
    ppermute x1, starting transfers between devices, body(): got = lax.ppermute(give, 'dp', swap)  14.7 us
    ppermute x1, waiting for transfers between devices, body(): back_last = lax.ppermute(theirs_last, 'dp', swap)  6.62 us
    all_to_all x1, starting transfers between devices, body(): lax.all_to_all(rows, 'expert', split_axis=0, concat_axis=0, tiled=True)  6.26 us
  transfers between devices with their start and end apart: 21, of which 13 were waited for; matrix products, arithmetic and copies ran while one was open for 0% of the time, Pallas kernels for 4%

profile of v3, /device:TPU:32, one launch (start us, length us, event | category | flops | bytes accessed | tf_op | source)
XLA Modules:
  0.0 234.1 jit_solution(17107683281365066140)
XLA Ops:
  6.5 1.1 broadcast_select_fusion.4
  7.6 14.7 %collective-permute-start = (bf16[48,2048]{1,0:T(8,128)(2,1)S(1)}, bf16[48,2048]{1,0:T(8,128)(2,1)S(1)}, u32[]{:S(2)}, u32[]{:S(2)}) collective-permute-start(bf16[48,2048]{1,0:T(8,128)(2,1)S(1)} %broadcast_select_fusion.4), channel_id=1, source_target_pairs={{0,32},{32,0},{64,96},{96,64},{128,160},{160,128},{192,224},{224,1... | collective-permute-start | bytes 589832 | tf_op jit(solution)/shard_map/ppermute | solution.py:186
  22.3 3.7 %collective-permute-done = bf16[48,2048]{1,0:T(8,128)(2,1)S(1)} collective-permute-done((bf16[48,2048]{1,0:T(8,128)(2,1)S(1)}, bf16[48,2048]{1,0:T(8,128)(2,1)S(1)}, u32[]{:S(2)}, u32[]{:S(2)}) %collective-permute-start) | collective-permute-done | bytes 196640 | tf_op jit(solution)/shard_map/ppermute | solution.py:186
  26.0 1.1 broadcast_select_fusion.3
  27.1 0.7 pad_maximum_fusion.1
  27.8 0.0 all-gather.2.cloned.1.call-update
  27.8 8.4 %collective-permute-start.1 = (bf16[96,768]{1,0:T(8,128)(2,1)S(1)}, bf16[96,768]{1,0:T(8,128)(2,1)S(1)}, u32[]{:S(2)}, u32[]{:S(2)}) collective-permute-start(bf16[96,768]{1,0:T(8,128)(2,1)S(1)} %pad_maximum_fusion.2.refs_5_), channel_id=1, source_target_pairs={{0,960},{32,992},{64,0},{96,32},{128,64},{160,96},{192,128},{224,1... | collective-permute-start | bytes 442376 | tf_op jit(solution)/shard_map/ppermute | solution.py:217
  36.2 1.9 collective-permute-start.3
  38.2 1.4 collective-permute-done.1.refs_6_
  39.5 6.5 %collective-permute-start.2 = (bf16[96,768]{1,0:T(8,128)(2,1)S(1)}, bf16[96,768]{1,0:T(8,128)(2,1)S(1)}, u32[]{:S(2)}, u32[]{:S(2)}) collective-permute-start(bf16[96,768]{1,0:T(8,128)(2,1)S(1)} %collective-permute-done.1.refs_6_), channel_id=1, source_target_pairs={{0,960},{32,992},{64,0},{96,32},{128,64},{160,96},{192,128},{224,1... | collective-permute-start | bytes 442376 | tf_op jit(solution)/shard_map/ppermute | solution.py:217
  46.1 1.6 collective-permute-done.3.refs_4_
  47.7 1.9 collective-permute-start.4
  49.6 0.0 copy-done.18
  49.6 3.3 %collective-permute-start.5 = (bf16[192,512]{1,0:T(8,128)(2,1)S(1)}, bf16[192,512]{1,0:T(8,128)(2,1)S(1)}, u32[]{:S(2)}, u32[]{:S(2)}) collective-permute-start(bf16[192,512]{1,0:T(8,128)(2,1)S(1)} %bitcast.9), channel_id=1, source_target_pairs={{0,32},{32,0},{64,96},{96,64},{128,160},{160,128},{192,224},{224,1... | collective-permute-start | bytes 589832 | tf_op jit(solution)/shard_map/ppermute | solution.py:200
  53.0 0.0 collective-permute-done.2.refs_7_
  53.0 6.0 %collective-permute-start.6 = (bf16[96,768]{1,0:T(8,128)(2,1)S(1)}, bf16[96,768]{1,0:T(8,128)(2,1)S(1)}, u32[]{:S(2)}, u32[]{:S(2)}) collective-permute-start(bf16[96,768]{1,0:T(8,128)(2,1)S(1)} %collective-permute-done.2.refs_7_), channel_id=1, source_target_pairs={{0,960},{32,992},{64,0},{96,32},{128,64},{160,96},{192,128},{224,1... | collective-permute-start | bytes 442376 | tf_op jit(solution)/shard_map/ppermute | solution.py:217
  59.0 0.0 collective-permute-done.4.refs_3_
  59.0 1.9 collective-permute-start.7
  61.0 0.1 copy.6.weights_ref
  61.1 0.1 copy.5.ids_ref
  61.3 21.9 %collective-permute-done.5.partner_ref = bf16[192,512]{1,0:T(8,128)(2,1)S(1)} collective-permute-done((bf16[192,512]{1,0:T(8,128)(2,1)S(1)}, bf16[192,512]{1,0:T(8,128)(2,1)S(1)}, u32[]{:S(2)}, u32[]{:S(2)}) %collective-permute-start.5) | collective-permute-done | bytes 196640 | tf_op jit(solution)/shard_map/ppermute | solution.py:200
  83.2 3.5 %shard_map.46 = bf16[8,384,256]{2,1,0:T(8,128)(2,1)} custom-call(s32[512,2]{1,0:T(8,128)S(1)} %copy.5.ids_ref, f32[512,2]{1,0:T(8,128)S(1)} %copy.6.weights_ref, bf16[192,512]{1,0:T(8,128)(2,1)S(1)} %bitcast.10, bf16[192,512]{1,0:T(8,128)(2,1)S(1)} %collective-permute-done.5.partner_ref), custom_call_target="tpu_custom_call" | custom-call | flops 805306368 | bytes 6291456 | tf_op jit(solution)/shard_map/pallas_call | solution.py:106
  86.7 0.0 collective-permute-done.6.refs_8_
  86.7 0.0 collective-permute-done.7.refs_2_
  86.7 6.3 %all-to-all-start = ((bf16[8,384,256]{2,1,0:T(8,128)(2,1)}), bf16[8,384,256]{2,1,0:T(8,128)(2,1)S(1)}, u32[]{:S(2)}, u32[]{:S(2)}) async-start(bf16[8,384,256]{2,1,0:T(8,128)(2,1)} %shard_map.46), calls=%async_computation | async-start | bytes 3145728 | tf_op jit(solution)/shard_map/all_to_all | solution.py:206
  93.0 1.9 collective-permute-start.10
  94.9 6.0 %collective-permute-start.8 = (bf16[96,768]{1,0:T(8,128)(2,1)S(1)}, bf16[96,768]{1,0:T(8,128)(2,1)S(1)}, u32[]{:S(2)}, u32[]{:S(2)}) collective-permute-start(bf16[96,768]{1,0:T(8,128)(2,1)S(1)} %collective-permute-done.6.refs_8_), channel_id=1, source_target_pairs={{0,960},{32,992},{64,0},{96,32},{128,64},{160,96},{192,128},{224,1... | collective-permute-start | bytes 442376 | tf_op jit(solution)/shard_map/ppermute | solution.py:217
  101.0 13.5 %collective-permute-done.10.refs_1_ = bf16[96,768]{1,0:T(8,128)(2,1)S(1)} collective-permute-done((bf16[96,768]{1,0:T(8,128)(2,1)S(1)}, bf16[96,768]{1,0:T(8,128)(2,1)S(1)}, u32[]{:S(2)}, u32[]{:S(2)}) %collective-permute-start.10) | collective-permute-done | bytes 147488 | tf_op jit(solution)/shard_map/ppermute | solution.py:215
  114.4 1.9 collective-permute-start.11
  116.3 0.7 copy-done.12
  117.0 0.0 collective-permute-done.8.refs_2_
  117.0 6.0 %collective-permute-start.9 = (bf16[96,768]{1,0:T(8,128)(2,1)S(1)}, bf16[96,768]{1,0:T(8,128)(2,1)S(1)}, u32[]{:S(2)}, u32[]{:S(2)}) collective-permute-start(bf16[96,768]{1,0:T(8,128)(2,1)S(1)} %collective-permute-done.8.refs_2_), channel_id=1, source_target_pairs={{0,960},{32,992},{64,0},{96,32},{128,64},{160,96},{192,128},{224,1... | collective-permute-start | bytes 442376 | tf_op jit(solution)/shard_map/ppermute | solution.py:217
  123.0 0.7 copy-done
  123.7 0.1 pad_add_fusion.base_ref
  123.8 8.8 %collective-permute-done.11.refs_9_ = bf16[96,768]{1,0:T(8,128)(2,1)S(1)} collective-permute-done((bf16[96,768]{1,0:T(8,128)(2,1)S(1)}, bf16[96,768]{1,0:T(8,128)(2,1)S(1)}, u32[]{:S(2)}, u32[]{:S(2)}) %collective-permute-start.11) | collective-permute-done | bytes 147488 | tf_op jit(solution)/shard_map/ppermute | solution.py:215
  132.5 2.6 %collective-permute-done.9.refs_3_ = bf16[96,768]{1,0:T(8,128)(2,1)S(1)} collective-permute-done((bf16[96,768]{1,0:T(8,128)(2,1)S(1)}, bf16[96,768]{1,0:T(8,128)(2,1)S(1)}, u32[]{:S(2)}, u32[]{:S(2)}) %collective-permute-start.9) | collective-permute-done | bytes 147488 | tf_op jit(solution)/shard_map/ppermute | solution.py:217
  135.2 0.7 copy-done.7
  135.9 0.0 all-to-all-done.rows_ref
  135.9 5.5 %shard_map.47 = (bf16[384,1536]{1,0:T(8,128)(2,1)S(1)}, bf16[384,1536]{1,0:T(8,128)(2,1)S(1)}) custom-call(s32[2]{0:T(128)S(1)} %pad_add_fusion.base_ref, bf16[8,384,256]{2,1,0:T(8,128)(2,1)S(1)} %all-to-all-done.rows_ref), custom_call_target="tpu_custom_call" | custom-call | flops 1207959552 | bytes 6291456 | tf_op jit(solution)/shard_map/pallas_call | solution.py:117
  141.4 0.0 copy-start.19
  141.4 7.0 %collective-permute-start.12 = (bf16[96,768]{1,0:T(8,128)(2,1)S(1)}, bf16[96,768]{1,0:T(8,128)(2,1)S(1)}, u32[]{:S(2)}, u32[]{:S(2)}) collective-permute-start(bf16[96,768]{1,0:T(8,128)(2,1)S(1)} %copy-done.8), channel_id=1, source_target_pairs={{0,960},{32,992},{64,0},{96,32},{128,64},{160,96},{192,128},{224,1... | collective-permute-start | bytes 442376 | tf_op jit(solution)/shard_map/ppermute | solution.py:217
  148.5 1.9 collective-permute-start.13
  150.4 10.5 %collective-permute-done.12.refs_4_ = bf16[96,768]{1,0:T(8,128)(2,1)S(1)} collective-permute-done((bf16[96,768]{1,0:T(8,128)(2,1)S(1)}, bf16[96,768]{1,0:T(8,128)(2,1)S(1)}, u32[]{:S(2)}, u32[]{:S(2)}) %collective-permute-start.12) | collective-permute-done | bytes 147488 | tf_op jit(solution)/shard_map/ppermute | solution.py:217
  160.9 0.7 copy-done.14
  161.6 5.7 %collective-permute-done.13.refs_8_ = bf16[96,768]{1,0:T(8,128)(2,1)S(1)} collective-permute-done((bf16[96,768]{1,0:T(8,128)(2,1)S(1)}, bf16[96,768]{1,0:T(8,128)(2,1)S(1)}, u32[]{:S(2)}, u32[]{:S(2)}) %collective-permute-start.13) | collective-permute-done | bytes 147488 | tf_op jit(solution)/shard_map/ppermute | solution.py:215
  167.4 0.9 copy-done.6
  168.3 0.9 copy-done.11
  169.2 0.9 copy-done.13
  170.1 0.6 shard_map.48.refs_0_
  170.8 1.9 collective-permute-start.14
  172.7 8.4 %collective-permute-done.14.refs_7_ = bf16[96,768]{1,0:T(8,128)(2,1)S(1)} collective-permute-done((bf16[96,768]{1,0:T(8,128)(2,1)S(1)}, bf16[96,768]{1,0:T(8,128)(2,1)S(1)}, u32[]{:S(2)}, u32[]{:S(2)}) %collective-permute-start.14) | collective-permute-done | bytes 147488 | tf_op jit(solution)/shard_map/ppermute | solution.py:215
  181.1 3.0 %collective-permute-start.15 = (bf16[96,768]{1,0:T(8,128)(2,1)S(1)}, bf16[96,768]{1,0:T(8,128)(2,1)S(1)}, u32[]{:S(2)}, u32[]{:S(2)}) collective-permute-start(bf16[96,768]{1,0:T(8,128)(2,1)S(1)} %collective-permute-done.14.refs_7_), channel_id=1, source_target_pairs={{0,64},{32,96},{64,128},{96,160},{128,192},{160,224},{192,256},{22... | collective-permute-start | bytes 442376 | tf_op jit(solution)/shard_map/ppermute | solution.py:215
  184.1 6.2 %collective-permute-done.15.refs_6_ = bf16[96,768]{1,0:T(8,128)(2,1)S(1)} collective-permute-done((bf16[96,768]{1,0:T(8,128)(2,1)S(1)}, bf16[96,768]{1,0:T(8,128)(2,1)S(1)}, u32[]{:S(2)}, u32[]{:S(2)}) %collective-permute-start.15) | collective-permute-done | bytes 147488 | tf_op jit(solution)/shard_map/ppermute | solution.py:215
  190.3 4.2 %convolution_convert_fusion = bf16[384,1280]{1,0:T(8,128)(2,1)S(1)} fusion(bf16[384,1536]{1,0:T(8,128)(2,1)} %copy-done.19, bf16[1536,1280]{1,0:T(8,128)(2,1)} %all-gather.2.cloned.1.call-done), kind=kOutput, calls=%fused_computation | convolution fusion | flops 1510440960 | bytes 6094848 | tf_op jit(solution)/shard_map/dot_general | solution.py:15
  194.5 0.1 fusion
  194.6 6.1 %collective-permute-start.17 = (bf16[192,1280]{1,0:T(8,128)(2,1)S(1)}, bf16[192,1280]{1,0:T(8,128)(2,1)S(1)}, u32[]{:S(2)}, u32[]{:S(2)}) collective-permute-start(bf16[192,1280]{1,0:T(8,128)(2,1)S(1)} %get-tuple-element.42), channel_id=1, source_target_pairs={{0,32},{32,0},{64,96},{96,64},{128,160},{160,128},{192,224},{224,1... | collective-permute-start | bytes 1474568 | tf_op jit(solution)/shard_map/ppermute | solution.py:223
  200.8 1.9 collective-permute-start.16
  202.7 13.6 %collective-permute-done.16.refs_5_ = bf16[96,768]{1,0:T(8,128)(2,1)S(1)} collective-permute-done((bf16[96,768]{1,0:T(8,128)(2,1)S(1)}, bf16[96,768]{1,0:T(8,128)(2,1)S(1)}, u32[]{:S(2)}, u32[]{:S(2)}) %collective-permute-start.16) | collective-permute-done | bytes 147488 | tf_op jit(solution)/shard_map/ppermute | solution.py:217
  216.3 0.6 shard_map.49
  217.0 1.9 collective-permute-start.18
  218.9 0.0 collective-permute-done.17
  219.0 6.6 %collective-permute-done.18 = bf16[192,768]{1,0:T(8,128)(2,1)S(1)} collective-permute-done((bf16[192,768]{1,0:T(8,128)(2,1)S(1)}, bf16[192,768]{1,0:T(8,128)(2,1)S(1)}, u32[]{:S(2)}, u32[]{:S(2)}) %collective-permute-start.18) | collective-permute-done | bytes 294944 | tf_op jit(solution)/shard_map/ppermute | solution.py:219
  225.6 0.3 broadcast_select_fusion.1
  226.0 1.3 maximum_bitcast_fusion
  (42 shorter events, 0.2 us)
Async XLA Ops:
  6.5 43.1 %copy-start.18 = (bf16[512,192]{0,1:T(8,128)(2,1)S(1)}, bf16[512,192]{0,1:T(8,128)(2,1)}, u32[]{:S(2)}) copy-start(bf16[512,192]{0,1:T(8,128)(2,1)} %param.4) | copy-start | bytes 589828
  6.5 54.4 %copy-start.20 = (f32[512,2]{0,1:T(2,128)S(1)}, f32[512,2]{0,1:T(2,128)}, u32[]{:S(2)}) copy-start(f32[512,2]{0,1:T(2,128)} %param.6) | copy-start | bytes 12292
  6.5 183.8 %all-gather.2.cloned.1.call-start = ((), (), s32[]{:S(2)}) async-start(), calls=%async_computation.1 | async-start | bytes 4177920 | tf_op jit(solution)/shard_map/all_gather | solution.py:190
  6.5 54.6 %copy-start.21 = (s32[512,2]{0,1:T(2,128)S(1)}, s32[512,2]{0,1:T(2,128)}, u32[]{:S(2)}) copy-start(s32[512,2]{0,1:T(2,128)} %param.5) | copy-start | bytes 12292
  7.6 18.4 %collective-permute-start = (bf16[48,2048]{1,0:T(8,128)(2,1)S(1)}, bf16[48,2048]{1,0:T(8,128)(2,1)S(1)}, u32[]{:S(2)}, u32[]{:S(2)}) collective-permute-start(bf16[48,2048]{1,0:T(8,128)(2,1)S(1)} %broadcast_select_fusion.4), channel_id=1, source_target_pairs={{0,32},{32,0},{64,96},{96,64},{128,160},{160,128},{192,224},{224,1... | collective-permute-start | bytes 589832 | tf_op jit(solution)/shard_map/ppermute | solution.py:186
  27.8 11.7 %collective-permute-start.1 = (bf16[96,768]{1,0:T(8,128)(2,1)S(1)}, bf16[96,768]{1,0:T(8,128)(2,1)S(1)}, u32[]{:S(2)}, u32[]{:S(2)}) collective-permute-start(bf16[96,768]{1,0:T(8,128)(2,1)S(1)} %pad_maximum_fusion.2.refs_5_), channel_id=1, source_target_pairs={{0,960},{32,992},{64,0},{96,32},{128,64},{160,96},{192,128},{224,1... | collective-permute-start | bytes 442376 | tf_op jit(solution)/shard_map/ppermute | solution.py:217
  36.2 11.5 %collective-permute-start.3 = (bf16[96,768]{1,0:T(8,128)(2,1)S(1)}, bf16[96,768]{1,0:T(8,128)(2,1)S(1)}, u32[]{:S(2)}, u32[]{:S(2)}) collective-permute-start(bf16[96,768]{1,0:T(8,128)(2,1)S(1)} %pad_maximum_fusion.2.refs_5_), channel_id=1, source_target_pairs={{0,64},{32,96},{64,128},{96,160},{128,192},{160,224},{192,256},{22... | collective-permute-start | bytes 442376 | tf_op jit(solution)/shard_map/ppermute | solution.py:215
  39.5 13.4 %collective-permute-start.2 = (bf16[96,768]{1,0:T(8,128)(2,1)S(1)}, bf16[96,768]{1,0:T(8,128)(2,1)S(1)}, u32[]{:S(2)}, u32[]{:S(2)}) collective-permute-start(bf16[96,768]{1,0:T(8,128)(2,1)S(1)} %collective-permute-done.1.refs_6_), channel_id=1, source_target_pairs={{0,960},{32,992},{64,0},{96,32},{128,64},{160,96},{192,128},{224,1... | collective-permute-start | bytes 442376 | tf_op jit(solution)/shard_map/ppermute | solution.py:217
  47.7 11.3 %collective-permute-start.4 = (bf16[96,768]{1,0:T(8,128)(2,1)S(1)}, bf16[96,768]{1,0:T(8,128)(2,1)S(1)}, u32[]{:S(2)}, u32[]{:S(2)}) collective-permute-start(bf16[96,768]{1,0:T(8,128)(2,1)S(1)} %collective-permute-done.3.refs_4_), channel_id=1, source_target_pairs={{0,64},{32,96},{64,128},{96,160},{128,192},{160,224},{192,256},{22... | collective-permute-start | bytes 442376 | tf_op jit(solution)/shard_map/ppermute | solution.py:215
  49.6 33.6 %collective-permute-start.5 = (bf16[192,512]{1,0:T(8,128)(2,1)S(1)}, bf16[192,512]{1,0:T(8,128)(2,1)S(1)}, u32[]{:S(2)}, u32[]{:S(2)}) collective-permute-start(bf16[192,512]{1,0:T(8,128)(2,1)S(1)} %bitcast.9), channel_id=1, source_target_pairs={{0,32},{32,0},{64,96},{96,64},{128,160},{160,128},{192,224},{224,1... | collective-permute-start | bytes 589832 | tf_op jit(solution)/shard_map/ppermute | solution.py:200
  53.0 33.7 %collective-permute-start.6 = (bf16[96,768]{1,0:T(8,128)(2,1)S(1)}, bf16[96,768]{1,0:T(8,128)(2,1)S(1)}, u32[]{:S(2)}, u32[]{:S(2)}) collective-permute-start(bf16[96,768]{1,0:T(8,128)(2,1)S(1)} %collective-permute-done.2.refs_7_), channel_id=1, source_target_pairs={{0,960},{32,992},{64,0},{96,32},{128,64},{160,96},{192,128},{224,1... | collective-permute-start | bytes 442376 | tf_op jit(solution)/shard_map/ppermute | solution.py:217
  59.0 27.7 %collective-permute-start.7 = (bf16[96,768]{1,0:T(8,128)(2,1)S(1)}, bf16[96,768]{1,0:T(8,128)(2,1)S(1)}, u32[]{:S(2)}, u32[]{:S(2)}) collective-permute-start(bf16[96,768]{1,0:T(8,128)(2,1)S(1)} %collective-permute-done.4.refs_3_), channel_id=1, source_target_pairs={{0,64},{32,96},{64,128},{96,160},{128,192},{160,224},{192,256},{22... | collective-permute-start | bytes 442376 | tf_op jit(solution)/shard_map/ppermute | solution.py:215
  86.7 8.2 %copy-start.5 = (bf16[96,768]{1,0:T(8,128)(2,1)}, bf16[96,768]{1,0:T(8,128)(2,1)S(1)}, u32[]{:S(2)}) copy-start(bf16[96,768]{1,0:T(8,128)(2,1)S(1)} %collective-permute-done.6.refs_8_) | copy-start | bytes 442372
  86.7 6.3 %copy-start.10 = (bf16[96,768]{1,0:T(8,128)(2,1)}, bf16[96,768]{1,0:T(8,128)(2,1)S(1)}, u32[]{:S(2)}) copy-start(bf16[96,768]{1,0:T(8,128)(2,1)S(1)} %collective-permute-done.7.refs_2_) | copy-start | bytes 442372
  86.7 49.1 %all-to-all-start = ((bf16[8,384,256]{2,1,0:T(8,128)(2,1)}), bf16[8,384,256]{2,1,0:T(8,128)(2,1)S(1)}, u32[]{:S(2)}, u32[]{:S(2)}) async-start(bf16[8,384,256]{2,1,0:T(8,128)(2,1)} %shard_map.46), calls=%async_computation | async-start | bytes 3145728 | tf_op jit(solution)/shard_map/all_to_all | solution.py:206
  93.0 21.4 %collective-permute-start.10 = (bf16[96,768]{1,0:T(8,128)(2,1)S(1)}, bf16[96,768]{1,0:T(8,128)(2,1)S(1)}, u32[]{:S(2)}, u32[]{:S(2)}) collective-permute-start(bf16[96,768]{1,0:T(8,128)(2,1)S(1)} %collective-permute-done.7.refs_2_), channel_id=1, source_target_pairs={{0,64},{32,96},{64,128},{96,160},{128,192},{160,224},{192,256},{22... | collective-permute-start | bytes 442376 | tf_op jit(solution)/shard_map/ppermute | solution.py:215
  94.9 22.1 %collective-permute-start.8 = (bf16[96,768]{1,0:T(8,128)(2,1)S(1)}, bf16[96,768]{1,0:T(8,128)(2,1)S(1)}, u32[]{:S(2)}, u32[]{:S(2)}) collective-permute-start(bf16[96,768]{1,0:T(8,128)(2,1)S(1)} %collective-permute-done.6.refs_8_), channel_id=1, source_target_pairs={{0,960},{32,992},{64,0},{96,32},{128,64},{160,96},{192,128},{224,1... | collective-permute-start | bytes 442376 | tf_op jit(solution)/shard_map/ppermute | solution.py:217
  114.4 18.1 %collective-permute-start.11 = (bf16[96,768]{1,0:T(8,128)(2,1)S(1)}, bf16[96,768]{1,0:T(8,128)(2,1)S(1)}, u32[]{:S(2)}, u32[]{:S(2)}) collective-permute-start(bf16[96,768]{1,0:T(8,128)(2,1)S(1)} %collective-permute-done.10.refs_1_), channel_id=1, source_target_pairs={{0,64},{32,96},{64,128},{96,160},{128,192},{160,224},{192,256},{22... | collective-permute-start | bytes 442376 | tf_op jit(solution)/shard_map/ppermute | solution.py:215
  116.3 0.7 copy-start.12
  117.0 18.2 %collective-permute-start.9 = (bf16[96,768]{1,0:T(8,128)(2,1)S(1)}, bf16[96,768]{1,0:T(8,128)(2,1)S(1)}, u32[]{:S(2)}, u32[]{:S(2)}) collective-permute-start(bf16[96,768]{1,0:T(8,128)(2,1)S(1)} %collective-permute-done.8.refs_2_), channel_id=1, source_target_pairs={{0,960},{32,992},{64,0},{96,32},{128,64},{160,96},{192,128},{224,1... | collective-permute-start | bytes 442376 | tf_op jit(solution)/shard_map/ppermute | solution.py:217
  123.0 0.7 copy-start
  132.5 2.6 %copy-start.2 = (bf16[96,768]{1,0:T(8,128)(2,1)}, bf16[96,768]{1,0:T(8,128)(2,1)S(1)}, u32[]{:S(2)}) copy-start(bf16[96,768]{1,0:T(8,128)(2,1)S(1)} %collective-permute-done.11.refs_9_) | copy-start | bytes 442372
  135.2 0.7 copy-start.7
  135.9 5.6 %copy-start.8 = (bf16[96,768]{1,0:T(8,128)(2,1)S(1)}, bf16[96,768]{1,0:T(8,128)(2,1)}, u32[]{:S(2)}) copy-start(bf16[96,768]{1,0:T(8,128)(2,1)} %copy-done.7) | copy-start | bytes 442372
  135.9 12.6 %copy-start.3 = (bf16[96,768]{1,0:T(8,128)(2,1)S(1)}, bf16[96,768]{1,0:T(8,128)(2,1)}, u32[]{:S(2)}) copy-start(bf16[96,768]{1,0:T(8,128)(2,1)} %copy-done.2) | copy-start | bytes 442372
  141.4 39.7 %copy-start.19 = (bf16[384,1536]{1,0:T(8,128)(2,1)}, bf16[384,1536]{1,0:T(8,128)(2,1)S(1)}, u32[]{:S(2)}) copy-start(bf16[384,1536]{1,0:T(8,128)(2,1)S(1)} %get-tuple-element.28) | copy-start | bytes 3538948
  141.4 19.5 %collective-permute-start.12 = (bf16[96,768]{1,0:T(8,128)(2,1)S(1)}, bf16[96,768]{1,0:T(8,128)(2,1)S(1)}, u32[]{:S(2)}, u32[]{:S(2)}) collective-permute-start(bf16[96,768]{1,0:T(8,128)(2,1)S(1)} %copy-done.8), channel_id=1, source_target_pairs={{0,960},{32,992},{64,0},{96,32},{128,64},{160,96},{192,128},{224,1... | collective-permute-start | bytes 442376 | tf_op jit(solution)/shard_map/ppermute | solution.py:217
  148.5 18.8 %collective-permute-start.13 = (bf16[96,768]{1,0:T(8,128)(2,1)S(1)}, bf16[96,768]{1,0:T(8,128)(2,1)S(1)}, u32[]{:S(2)}, u32[]{:S(2)}) collective-permute-start(bf16[96,768]{1,0:T(8,128)(2,1)S(1)} %copy-done.3), channel_id=1, source_target_pairs={{0,64},{32,96},{64,128},{96,160},{128,192},{160,224},{192,256},{22... | collective-permute-start | bytes 442376 | tf_op jit(solution)/shard_map/ppermute | solution.py:215
  160.9 0.7 copy-start.14
  167.3 3.4 %copy-start.16 = (bf16[96,768]{1,0:T(8,128)(2,1)}, bf16[96,768]{1,0:T(8,128)(2,1)S(1)}, u32[]{:S(2)}) copy-start(bf16[96,768]{1,0:T(8,128)(2,1)S(1)} %collective-permute-done.13.refs_8_) | copy-start | bytes 442372
  167.3 0.9 copy-start.6
  168.3 0.9 copy-start.11
  169.2 0.9 copy-start.13
  170.8 10.3 %collective-permute-start.14 = (bf16[96,768]{1,0:T(8,128)(2,1)S(1)}, bf16[96,768]{1,0:T(8,128)(2,1)S(1)}, u32[]{:S(2)}, u32[]{:S(2)}) collective-permute-start(bf16[96,768]{1,0:T(8,128)(2,1)S(1)} %collective-permute-done.13.refs_8_), channel_id=1, source_target_pairs={{0,64},{32,96},{64,128},{96,160},{128,192},{160,224},{192,256},{22... | collective-permute-start | bytes 442376 | tf_op jit(solution)/shard_map/ppermute | solution.py:215
  181.1 9.2 %collective-permute-start.15 = (bf16[96,768]{1,0:T(8,128)(2,1)S(1)}, bf16[96,768]{1,0:T(8,128)(2,1)S(1)}, u32[]{:S(2)}, u32[]{:S(2)}) collective-permute-start(bf16[96,768]{1,0:T(8,128)(2,1)S(1)} %collective-permute-done.14.refs_7_), channel_id=1, source_target_pairs={{0,64},{32,96},{64,128},{96,160},{128,192},{160,224},{192,256},{22... | collective-permute-start | bytes 442376 | tf_op jit(solution)/shard_map/ppermute | solution.py:215
  194.5 6.3 %copy-start.15 = (bf16[96,768]{1,0:T(8,128)(2,1)S(1)}, bf16[96,768]{1,0:T(8,128)(2,1)}, u32[]{:S(2)}) copy-start(bf16[96,768]{1,0:T(8,128)(2,1)} %copy-done.14) | copy-start | bytes 442372
  194.5 21.8 %copy-start.1 = (bf16[96,768]{1,0:T(8,128)(2,1)S(1)}, bf16[96,768]{1,0:T(8,128)(2,1)}, u32[]{:S(2)}) copy-start(bf16[96,768]{1,0:T(8,128)(2,1)} %copy-done) | copy-start | bytes 442372
  194.5 21.8 %copy-start.4 = (bf16[96,768]{1,0:T(8,128)(2,1)S(1)}, bf16[96,768]{1,0:T(8,128)(2,1)}, u32[]{:S(2)}) copy-start(bf16[96,768]{1,0:T(8,128)(2,1)} %copy-done.2) | copy-start | bytes 442372
  194.5 21.8 %copy-start.9 = (bf16[96,768]{1,0:T(8,128)(2,1)S(1)}, bf16[96,768]{1,0:T(8,128)(2,1)}, u32[]{:S(2)}) copy-start(bf16[96,768]{1,0:T(8,128)(2,1)} %copy-done.7) | copy-start | bytes 442372
  194.5 21.8 %copy-start.17 = (bf16[96,768]{1,0:T(8,128)(2,1)S(1)}, bf16[96,768]{1,0:T(8,128)(2,1)}, u32[]{:S(2)}) copy-start(bf16[96,768]{1,0:T(8,128)(2,1)} %copy-done.16) | copy-start | bytes 442372
  194.6 24.3 %collective-permute-start.17 = (bf16[192,1280]{1,0:T(8,128)(2,1)S(1)}, bf16[192,1280]{1,0:T(8,128)(2,1)S(1)}, u32[]{:S(2)}, u32[]{:S(2)}) collective-permute-start(bf16[192,1280]{1,0:T(8,128)(2,1)S(1)} %get-tuple-element.42), channel_id=1, source_target_pairs={{0,32},{32,0},{64,96},{96,64},{128,160},{160,128},{192,224},{224,1... | collective-permute-start | bytes 1474568 | tf_op jit(solution)/shard_map/ppermute | solution.py:223
  200.8 15.6 %collective-permute-start.16 = (bf16[96,768]{1,0:T(8,128)(2,1)S(1)}, bf16[96,768]{1,0:T(8,128)(2,1)S(1)}, u32[]{:S(2)}, u32[]{:S(2)}) collective-permute-start(bf16[96,768]{1,0:T(8,128)(2,1)S(1)} %copy-done.15), channel_id=1, source_target_pairs={{0,960},{32,992},{64,0},{96,32},{128,64},{160,96},{192,128},{224,1... | collective-permute-start | bytes 442376 | tf_op jit(solution)/shard_map/ppermute | solution.py:217
  217.0 8.6 %collective-permute-start.18 = (bf16[192,768]{1,0:T(8,128)(2,1)S(1)}, bf16[192,768]{1,0:T(8,128)(2,1)S(1)}, u32[]{:S(2)}, u32[]{:S(2)}) collective-permute-start(bf16[192,768]{1,0:T(8,128)(2,1)S(1)} %get-tuple-element.38), channel_id=1, source_target_pairs={{0,32},{32,0},{64,96},{96,64},{128,160},{160,128},{192,224},{224,1... | collective-permute-start | bytes 884744 | tf_op jit(solution)/shard_map/ppermute | solution.py:219
Sparse Core Ops, SparseCore 0:
  27.9 142.3 all-gather.1

commit v4 on v2

--- a/solution.py
+++ b/solution.py
@@ -25,26 +25,39 @@
     return earlier + later
 
 
-def product_kernel(left_ref, right_ref, out_ref):
-    out_ref[...] = jnp.dot(
-        left_ref[...], right_ref[...], preferred_element_type=jnp.float32
-    ).astype(out_ref.dtype)
+def product_kernel(left_ref, right_ref, out_ref, held, arrived):
+    blocks = arrived.shape[0]
+    width = held.shape[1] // blocks
+    spans = [slice(i * width, (i + 1) * width) for i in range(blocks)]
+    copies = [
+        pltpu.make_async_copy(right_ref.at[:, span], held.at[:, span], arrived.at[i])
+        for i, span in enumerate(spans)
+    ]
+    for copy in copies:
+        copy.start()
+    for copy, span in zip(copies, spans):
+        copy.wait()
+        out_ref[:, span] = jnp.dot(
+            left_ref[...], held[:, span], preferred_element_type=jnp.float32
+        ).astype(out_ref.dtype)
 
 
 def product(left, right):
     rows, depth = left.shape
     columns = right.shape[1]
-    width = 512
     return pl.pallas_call(
         product_kernel,
         out_shape=jax.ShapeDtypeStruct((rows, columns), jnp.bfloat16),
-        grid=(columns // width,),
         in_specs=[
-            pl.BlockSpec((rows, depth), lambda i: (0, 0)),
-            pl.BlockSpec((depth, width), lambda i: (0, i)),
+            pl.BlockSpec(memory_space=pltpu.VMEM),
+            pl.BlockSpec(memory_space=pl.ANY),
         ],
-        out_specs=pl.BlockSpec((rows, width), lambda i: (0, i)),
-        compiler_params=pltpu.CompilerParams(vmem_limit_bytes=16 << 20),
+        out_specs=pl.BlockSpec(memory_space=pltpu.VMEM),
+        scratch_shapes=[
+            pltpu.VMEM((depth, columns), jnp.bfloat16),
+            pltpu.SemaphoreType.DMA((8,)),
+        ],
+        compiler_params=pltpu.CompilerParams(vmem_limit_bytes=56 << 20),
         cost_estimate=pl.CostEstimate(
             flops=2 * rows * depth * columns,
             bytes_accessed=2 * (rows * depth + depth * columns + rows * columns),

time: 204 us -> 201 us (0.985)
  local copies, waits for them, and re-layouts: 23.8 us -> 20.3 us
    unnamed x8 -> x6, local copies, waits for them, and re-layouts: 8.07 us -> 4.34 us
  transfers between devices with their start and end apart: 3 -> 3, of which waited for: 2 -> 2; matrix products, arithmetic and copies ran while one was open for 14% -> 15% of each run, Pallas kernels for 0% -> 0%
where the time goes in v4:
time: 201 us; the launch traced here: 200 us
  waiting for transfers between devices  131 us (65%)
  local copies, waits for them, and re-layouts  20.3 us (10%)
  between operations  14.2 us (7%)
  other arithmetic  9.93 us (5%)
  blocking collectives  9.22 us (5%)
  starting transfers between devices  8.04 us (4%)
  Pallas kernels  7.65 us (4%)
    all_gather x1, waiting for transfers between devices, body(): gathered = lax.all_gather(hidden[0], 'dp', axis=0, tiled=True)  117 us
    all_to_all x1, waiting for transfers between devices, body(): lax.all_to_all(send_rows, 'expert', split_axis=0, concat_axis=0, tiled=True)  13 us
    unnamed x1, blocking collectives  9.22 us
    pallas_call x1, Pallas kernels, product(): pl.pallas_call(product_kernel, out_shape=jax.ShapeDtypeStruct((rows, colu...  7.65 us
    scatter x1, local copies, waits for them, and re-layouts, body(): arranged.at[arrived_slots.reshape(-1)]  7.47 us
    scatter x1, other arithmetic, body(): jnp.zeros((experts * block_most, features), jnp.bfloat16).at[send_index]  6.33 us
    all_to_all x1, starting transfers between devices, body(): lax.all_to_all(send_rows, 'expert', split_axis=0, concat_axis=0, tiled=True)  4.72 us
    unnamed x6, local copies, waits for them, and re-layouts  4.34 us
  transfers between devices with their start and end apart: 3, of which 2 were waited for; matrix products, arithmetic and copies ran while one was open for 15% of the time, Pallas kernels for 0%

profile of v4, /device:TPU:24, one launch (start us, length us, event | category | flops | bytes accessed | tf_op | source)
XLA Modules:
  0.0 200.5 jit_solution(11005548999673610137)
XLA Ops:
  6.5 0.0 all-gather.4.cloned.1.call-start
  6.5 0.7 all-gather.4.cloned.1.call-update
  7.3 0.8 copy.6
  8.1 0.2 eq.25
  8.3 0.2 eq.29
  8.5 0.7 broadcast_multiply_fusion
  9.1 0.1 copy.5
  9.3 0.2 mul.47
  9.5 1.3 dynamic-slice
  11.5 0.1 convert_reduce_fusion
  11.6 0.2 dynamic-update-slice
  11.9 9.2 %all-reduce = s32[64]{0:T(128)S(1)} all-reduce(s32[64]{0:T(128)S(1)} %dynamic-update-slice), channel_id=2, replica_groups=mesh['dp'=32,'expert'=8,'tensor'=4] {'expert'}, use_global_device_ids=true, to_apply=%add | all-reduce | flops 64 | bytes 512
  21.1 0.1 reshape.124
  21.2 2.3 %reduce-window.6 = s32[8,8,128]{2,1,0:T(8,128)S(1)} reduce-window(s32[8,8,128]{2,1,0:T(8,128)S(1)} %fusion.7, s32[]{:T(128)} %constant.44.clone.1), window={size=1x1x128 pad=0_0x0_0x127_0}, to_apply=%region_0.0 | reduce-window | flops 1040384 | bytes 65540 | tf_op jit(solution)/shard_map/reduce-window
  23.5 0.3 slice_reduce_fusion
  23.7 0.2 reduce-window.9
  23.9 0.1 add_bitcast_fusion
  24.0 0.3 while.14
  24.3 0.1 select_reduce_fusion
  24.4 4.3 %scatter_custom_fusion = s32[1536]{0:T(1024)S(1)} fusion(s32[1024]{0:T(1024)S(1)} %bitcast.33, s32[1024]{0:T(1024)S(1)} %add.67, s32[]{:T(128)} %constant.42.clone.1), kind=kCustom, calls=%fused_computation.25 | custom fusion | bytes 6148 | tf_op jit(solution)/shard_map/scatter | solution.py:89
  28.7 0.7 all_to_all.9
  29.4 3.3 %all-to-all-start = ((s32[8,1,192]{2,1,0:T(1,128)}), s32[8,1,192]{2,1,0:T(1,128)S(1)}, u32[]{:S(2)}, u32[]{:S(2)}) async-start(s32[8,1,192]{2,1,0:T(1,128)} %all_to_all.9), calls=%async_computation | async-start | bytes 16384 | tf_op jit(solution)/shard_map/all_to_all | solution.py:95
  32.7 0.8 copy.8
  33.6 0.2 mul.51
  33.7 1.1 copy.9
  34.8 0.4 mul.53
  35.2 0.7 mul.54
  35.9 6.3 %scatter_custom_fusion.1 = bf16[1536,192]{1,0:T(8,128)(2,1)} fusion(s32[1024]{0:T(1024)S(1)} %bitcast.34, f32[1024,192]{1,0:T(8,128)S(1)} %mul.54, f32[1024]{0:T(1024)S(1)} %mul.51, bf16[]{:T(256)} %constant.41.clone.1), kind=kCustom, calls=%fused_computation.6 | custom fusion | flops 393216 | bytes 1642498 | tf_op jit(solution)/shard_map/scatter | solution.py:87
  42.2 0.0 all-to-all-done
  42.2 4.7 %all-to-all-start.1 = ((bf16[8,192,192]{2,1,0:T(8,128)(2,1)}), bf16[8,192,192]{2,1,0:T(8,128)(2,1)S(1)}, u32[]{:S(2)}, u32[]{:S(2)}) async-start(bf16[8,192,192]{2,1,0:T(8,128)(2,1)} %bitcast.4), calls=%async_computation.1 | async-start | bytes 1572864 | tf_op jit(solution)/shard_map/all_to_all | solution.py:94
  47.0 0.1 reshape.97
  47.1 13.0 %all-to-all-done.1 = bf16[8,192,192]{2,1,0:T(8,128)(2,1)S(1)} async-done(((bf16[8,192,192]{2,1,0:T(8,128)(2,1)}), bf16[8,192,192]{2,1,0:T(8,128)(2,1)S(1)}, u32[]{:S(2)}, u32[]{:S(2)}) %all-to-all-start.1) | async-done | bytes 589856 | tf_op jit(solution)/shard_map/all_to_all | solution.py:94
  60.1 7.5 %scatter_custom_fusion.2 = bf16[1537,192]{1,0:T(8,128)(2,1)S(1)} fusion(s32[1536]{0:T(1024)S(1)} %fusion.8, bf16[1536,192]{1,0:T(8,128)(2,1)S(1)} %bitcast.30, bf16[]{:T(256)} %constant.41.clone.1), kind=kCustom, calls=%fused_computation.8 | custom fusion | bytes 590210 | tf_op jit(solution)/shard_map/scatter | solution.py:98
  67.6 0.1 slice.13
  67.6 1.1 copy.11
  68.7 117.2 %all-gather.4.cloned.1.call-done = bf16[1,1536,4096]{2,1,0:T(8,128)(2,1)} async-done(((bf16[1,48,4096]{2,1,0:T(8,128)(2,1)}), bf16[1,1536,4096]{2,1,0:T(8,128)(2,1)}) %all-gather.4.cloned.1.call-update) | async-done | bytes 12582928 | tf_op jit(solution)/shard_map/all_gather | solution.py:101
  185.9 7.7 %shard_map.46 = bf16[192,4096]{1,0:T(8,128)(2,1)} custom-call(bf16[192,1536]{1,0:T(8,128)(2,1)} %bitcast.29, bf16[1536,4096]{1,0:T(8,128)(2,1)} %bitcast.28), custom_call_target="tpu_custom_call" | custom-call | flops 2415919104 | bytes 14745600 | tf_op jit(solution)/shard_map/pallas_call | solution.py:48
  (15 shorter events, 0.2 us)
Async XLA Ops:
  6.5 179.4 %all-gather.4.cloned.1.call-start = ((), (), s32[]{:S(2)}) async-start(), calls=%async_computation.2 | async-start | bytes 12976128 | tf_op jit(solution)/shard_map/all_gather | solution.py:101
  29.4 12.8 %all-to-all-start = ((s32[8,1,192]{2,1,0:T(1,128)}), s32[8,1,192]{2,1,0:T(1,128)S(1)}, u32[]{:S(2)}, u32[]{:S(2)}) async-start(s32[8,1,192]{2,1,0:T(1,128)} %all_to_all.9), calls=%async_computation | async-start | bytes 16384 | tf_op jit(solution)/shard_map/all_to_all | solution.py:95
  42.2 17.9 %all-to-all-start.1 = ((bf16[8,192,192]{2,1,0:T(8,128)(2,1)}), bf16[8,192,192]{2,1,0:T(8,128)(2,1)S(1)}, u32[]{:S(2)}, u32[]{:S(2)}) async-start(bf16[8,192,192]{2,1,0:T(8,128)(2,1)} %bitcast.4), calls=%async_computation.1 | async-start | bytes 1572864 | tf_op jit(solution)/shard_map/all_to_all | solution.py:94
Sparse Core Ops, SparseCore 0:
  10.0 175.8 all-gather.3

commit v5 on v4

--- a/solution.py
+++ b/solution.py
@@ -6,6 +6,7 @@
 from jax.sharding import PartitionSpec as P
 
 TOP = 2
+SMALL = (256, 256)
 
 
 def prefix(array, axis, combine, identity):
@@ -25,7 +26,8 @@
     return earlier + later
 
 
-def product_kernel(left_ref, right_ref, out_ref, held, arrived):
+def product_kernel(left_ref, right_ref, *refs):
+    *parts, out_ref, held, arrived = refs
     blocks = arrived.shape[0]
     width = held.shape[1] // blocks
     spans = [slice(i * width, (i + 1) * width) for i in range(blocks)]
@@ -35,6 +37,10 @@
     ]
     for copy in copies:
         copy.start()
+    start = held.shape[1]
+    for part in parts:
+        out_ref[:, start : start + part.shape[1]] = part[...]
+        start += part.shape[1]
     for copy, span in zip(copies, spans):
         copy.wait()
         out_ref[:, span] = jnp.dot(
@@ -42,20 +48,22 @@
         ).astype(out_ref.dtype)
 
 
-def product(left, right):
+def product(left, right, parts):
     rows, depth = left.shape
     columns = right.shape[1]
+    width = columns + sum(part.shape[1] for part in parts)
     return pl.pallas_call(
         product_kernel,
-        out_shape=jax.ShapeDtypeStruct((rows, columns), jnp.bfloat16),
+        out_shape=jax.ShapeDtypeStruct((rows, width), jnp.bfloat16),
         in_specs=[
             pl.BlockSpec(memory_space=pltpu.VMEM),
             pl.BlockSpec(memory_space=pl.ANY),
+            *[pl.BlockSpec(memory_space=pltpu.VMEM)] * len(parts),
         ],
         out_specs=pl.BlockSpec(memory_space=pltpu.VMEM),
         scratch_shapes=[
             pltpu.VMEM((depth, columns), jnp.bfloat16),
-            pltpu.SemaphoreType.DMA((8,)),
+            pltpu.SemaphoreType.DMA((columns // 512,)),
         ],
         compiler_params=pltpu.CompilerParams(vmem_limit_bytes=56 << 20),
         cost_estimate=pl.CostEstimate(
@@ -63,7 +71,7 @@
             bytes_accessed=2 * (rows * depth + depth * columns + rows * columns),
             transcendentals=0,
         ),
-    )(left, right)
+    )(left, right, *parts)
 
 
 def body(out_grad, expert_ids, combine, hidden):
@@ -98,8 +106,21 @@
     arranged = arranged.at[arrived_slots.reshape(-1)].set(arrived_rows.reshape(-1, features))[
         :capacity
     ]
-    gathered = lax.all_gather(hidden[0], "dp", axis=0, tiled=True)
-    return product(arranged.T, gathered).T[None]
+    hidden = hidden[0]
+    most = hidden.shape[1] - sum(SMALL)
+    gathered = lax.all_gather(hidden[:, :most], "dp", axis=0, tiled=True)
+    parts, start = [], most
+    for width in SMALL:
+        some = lax.all_gather(hidden[:, start : start + width], "dp", axis=0, tiled=True)
+        parts.append(dot(arranged, some))
+        start += width
+    return product(arranged.T, gathered, parts).T[None]
+
+
+def dot(left, right):
+    return lax.dot_general(
+        left, right, (((0,), (0,)), ((), ())), preferred_element_type=jnp.float32
+    ).astype(jnp.bfloat16)
 
 
 def solution(mesh):

time: 201 us -> 213 us (1.060)
  blocking collectives: 9.22 us -> 147 us
  waiting for transfers between devices: 131 us -> 0.02 us
  local copies, waits for them, and re-layouts: 20.3 us -> 22.7 us
  matrix products: 0 us -> 2.17 us
    all_gather x0 -> x2, blocking collectives: none -> 138 us  [body(): lax.all_gather(hidden[:, start:start + width], 'dp', axis=0, tiled=True)]
    all_gather x1, waiting for transfers between devices: 117 us -> 0.01 us  [body(): gathered = lax.all_gather(hidden[:, :most], 'dp', axis=0, tiled=True)]
    all_to_all x1, waiting for transfers between devices: 13 us -> 0.01 us  [body(): lax.all_to_all(send_rows, 'expert', split_axis=0, concat_axis=0, tiled=True)]
    slice x2 -> x3, local copies, waits for them, and re-layouts: 0.33 us -> 2.78 us  [the longest x1 1.74 us: body(): gathered = lax.all_gather(hidden[:, :most], 'dp', axis=0, tiled=True)]
    dot_general x0 -> x2, matrix products: none -> 2.17 us  [dot(): lax.dot_general(left, right, (((0,), (0,)), ((), ())), preferred_element_...]
    unnamed x6 -> x7, local copies, waits for them, and re-layouts: 4.34 us -> 4.27 us
  transfers between devices with their start and end apart: 3 -> 3, of which waited for: 2 -> 0; matrix products, arithmetic and copies ran while one was open for 15% -> 15% of each run, Pallas kernels for 0% -> 0%
where the time goes in v5:
time: 213 us; the launch traced here: 211 us
  blocking collectives  147 us (69%)
  local copies, waits for them, and re-layouts  22.7 us (11%)
  between operations  14.1 us (7%)
  other arithmetic  9.93 us (5%)
  starting transfers between devices  7.99 us (4%)
  Pallas kernels  7.1 us (3%)
  matrix products  2.17 us (1%)
    all_gather x2, blocking collectives, body(): lax.all_gather(hidden[:, start:start + width], 'dp', axis=0, tiled=True)  138 us
    unnamed x1, blocking collectives  9.22 us
    scatter x1, local copies, waits for them, and re-layouts, body(): arranged.at[arrived_slots.reshape(-1)]  7.47 us
    pallas_call x1, Pallas kernels, product(): pl.pallas_call(product_kernel, out_shape=jax.ShapeDtypeStruct((rows, widt...  7.1 us
    scatter x1, other arithmetic, body(): jnp.zeros((experts * block_most, features), jnp.bfloat16).at[send_index]  6.33 us
    all_to_all x1, starting transfers between devices, body(): lax.all_to_all(send_rows, 'expert', split_axis=0, concat_axis=0, tiled=True)  4.72 us
    scatter x1, local copies, waits for them, and re-layouts, body(): jnp.full((experts * block_most,), capacity, jnp.int32).at[send_index]  4.32 us
    unnamed x7, local copies, waits for them, and re-layouts  4.27 us
  transfers between devices with their start and end apart: 3, of which 0 were waited for; matrix products, arithmetic and copies ran while one was open for 15% of the time, Pallas kernels for 0%

profile of v5, /device:TPU:24, one launch (start us, length us, event | category | flops | bytes accessed | tf_op | source)
XLA Modules:
  0.0 211.3 jit_solution(17262777218757831486)
XLA Ops:
  6.5 0.0 all-gather.3.cloned.1.call-start
  6.5 1.7 slice.26
  8.3 0.0 all-gather.3.cloned.1.call-update
  8.3 0.8 copy.6
  9.1 0.2 eq.29
  9.3 0.2 eq.25
  9.5 2.3 %reduce-window.6 = s32[8,8,128]{2,1,0:T(8,128)S(1)} reduce-window(s32[8,8,128]{2,1,0:T(8,128)S(1)} %fusion.7, s32[]{:T(128)} %constant.44.clone.1), window={size=1x1x128 pad=0_0x0_0x127_0}, to_apply=%region_0.0 | reduce-window | flops 1040384 | bytes 65540 | tf_op jit(solution)/shard_map/reduce-window
  11.8 0.3 slice_reduce_fusion
  12.1 0.2 reduce-window.9
  12.2 1.2 dynamic-slice
  14.0 0.1 convert_reduce_fusion
  14.1 0.2 dynamic-update-slice
  14.4 9.2 %all-reduce = s32[64]{0:T(128)S(1)} all-reduce(s32[64]{0:T(128)S(1)} %dynamic-update-slice), channel_id=2, replica_groups=mesh['dp'=32,'expert'=8,'tensor'=4] {'expert'}, use_global_device_ids=true, to_apply=%add | all-reduce | flops 64 | bytes 512
  23.6 0.1 reshape.124
  23.7 0.7 broadcast_multiply_fusion
  24.4 0.1 copy.5
  24.5 0.2 mul.47
  24.7 0.1 add_bitcast_fusion
  24.8 0.3 while.14
  25.1 0.1 select_reduce_fusion
  25.2 4.3 %scatter_custom_fusion = s32[1536]{0:T(1024)S(1)} fusion(s32[1024]{0:T(1024)S(1)} %bitcast.33, s32[1024]{0:T(1024)S(1)} %add.67, s32[]{:T(128)} %constant.42.clone.1), kind=kCustom, calls=%fused_computation.27 | custom fusion | bytes 6148 | tf_op jit(solution)/shard_map/scatter | solution.py:97
  29.5 0.7 all_to_all.9
  30.2 3.3 %all-to-all-start = ((s32[8,1,192]{2,1,0:T(1,128)}), s32[8,1,192]{2,1,0:T(1,128)S(1)}, u32[]{:S(2)}, u32[]{:S(2)}) async-start(s32[8,1,192]{2,1,0:T(1,128)} %all_to_all.9), calls=%async_computation | async-start | bytes 16384 | tf_op jit(solution)/shard_map/all_to_all | solution.py:103
  33.5 0.8 fusion.13
  34.3 1.1 copy.9
  35.3 0.4 mul.53
  35.7 0.7 mul.54
  36.4 0.8 copy.8
  37.2 0.2 mul.51
  37.4 6.3 %scatter_custom_fusion.1 = bf16[1536,192]{1,0:T(8,128)(2,1)} fusion(s32[1024]{0:T(1024)S(1)} %bitcast.34, f32[1024,192]{1,0:T(8,128)S(1)} %mul.54, f32[1024]{0:T(1024)S(1)} %mul.51, bf16[]{:T(256)} %constant.41.clone.1), kind=kCustom, calls=%fused_computation.8 | custom fusion | flops 393216 | bytes 1642498 | tf_op jit(solution)/shard_map/scatter | solution.py:95
  43.7 0.0 all-to-all-done
  43.7 4.7 %all-to-all-start.1 = ((bf16[8,192,192]{2,1,0:T(8,128)(2,1)}), bf16[8,192,192]{2,1,0:T(8,128)(2,1)S(1)}, u32[]{:S(2)}, u32[]{:S(2)}) async-start(bf16[8,192,192]{2,1,0:T(8,128)(2,1)} %bitcast.4), calls=%async_computation.1 | async-start | bytes 1572864 | tf_op jit(solution)/shard_map/all_to_all | solution.py:102
  48.5 76.8 %all_gather.19 = bf16[1536,256]{1,0:T(8,128)(2,1)S(1)} all-gather(bf16[48,256]{1,0:T(8,128)(2,1)S(1)} %get-tuple-element.110), channel_id=1, replica_groups=mesh['dp'=32,'expert'=8,'tensor'=4] {'dp'}, dimensions={0}, use_global_device_ids=true | all-gather | bytes 811008 | tf_op jit(solution)/shard_map/all_gather | solution.py:114
  125.2 61.2 %all_gather.18 = bf16[1536,256]{1,0:T(8,128)(2,1)S(1)} all-gather(bf16[48,256]{1,0:T(8,128)(2,1)S(1)} %get-tuple-element.111), channel_id=1, replica_groups=mesh['dp'=32,'expert'=8,'tensor'=4] {'dp'}, dimensions={0}, use_global_device_ids=true | all-gather | bytes 811008 | tf_op jit(solution)/shard_map/all_gather | solution.py:114
  186.5 0.1 reshape.97
  186.6 0.0 all-to-all-done.1
  186.6 7.5 %scatter_custom_fusion.2 = bf16[1537,192]{1,0:T(8,128)(2,1)S(1)} fusion(s32[1536]{0:T(1024)S(1)} %fusion.8, bf16[1536,192]{1,0:T(8,128)(2,1)S(1)} %bitcast.28, bf16[]{:T(256)} %constant.41.clone.1), kind=kCustom, calls=%fused_computation.10 | custom fusion | bytes 590210 | tf_op jit(solution)/shard_map/scatter | solution.py:106
  194.1 0.1 slice.25
  194.1 1.1 copy.11
  195.2 1.1 convolution_convert_fusion.refs_1_
  196.3 1.1 convolution_convert_fusion.1.refs_0_
  197.4 0.0 all-gather.3.cloned.1.call-done.right_ref
  197.4 7.1 %shard_map.46 = bf16[192,4096]{1,0:T(8,128)(2,1)} custom-call(bf16[192,1536]{1,0:T(8,128)(2,1)} %bitcast.27, bf16[1536,3584]{1,0:T(8,128)(2,1)} %all-gather.3.cloned.1.call-done.right_ref, bf16[192,256]{1,0:T(8,128)(2,1)} %convolution_convert_fusion.1.refs_0_, bf16[192,256]{1,0:T(8,128)(2,1)} %convolution_convert_fusion.refs_1_), custom_call_target="tpu_custom_call" | custom-call | flops 2113929216 | bytes 12976128 | tf_op jit(solution)/shard_map/pallas_call | solution.py:55
  (15 shorter events, 0.2 us)
Async XLA Ops:
  6.5 190.8 %all-gather.3.cloned.1.call-start = ((), (), s32[]{:S(2)}) async-start(), calls=%async_computation.2 | async-start | bytes 11354112 | tf_op jit(solution)/shard_map/all_gather | solution.py:111
  30.2 13.5 %all-to-all-start = ((s32[8,1,192]{2,1,0:T(1,128)}), s32[8,1,192]{2,1,0:T(1,128)S(1)}, u32[]{:S(2)}, u32[]{:S(2)}) async-start(s32[8,1,192]{2,1,0:T(1,128)} %all_to_all.9), calls=%async_computation | async-start | bytes 16384 | tf_op jit(solution)/shard_map/all_to_all | solution.py:103
  43.7 142.8 %all-to-all-start.1 = ((bf16[8,192,192]{2,1,0:T(8,128)(2,1)}), bf16[8,192,192]{2,1,0:T(8,128)(2,1)S(1)}, u32[]{:S(2)}, u32[]{:S(2)}) async-start(bf16[8,192,192]{2,1,0:T(8,128)(2,1)} %bitcast.4), calls=%async_computation.1 | async-start | bytes 1572864 | tf_op jit(solution)/shard_map/all_to_all | solution.py:102
Sparse Core Ops, SparseCore 0:
  10.0 178.1 all-gather.2

commit v6 on v5

--- a/solution.py
+++ b/solution.py
@@ -6,7 +6,7 @@
 from jax.sharding import PartitionSpec as P
 
 TOP = 2
-SMALL = (256, 256)
+SMALL = (256,)
 
 
 def prefix(array, axis, combine, identity):
@@ -63,7 +63,7 @@
         out_specs=pl.BlockSpec(memory_space=pltpu.VMEM),
         scratch_shapes=[
             pltpu.VMEM((depth, columns), jnp.bfloat16),
-            pltpu.SemaphoreType.DMA((columns // 512,)),
+            pltpu.SemaphoreType.DMA((columns // 640,)),
         ],
         compiler_params=pltpu.CompilerParams(vmem_limit_bytes=56 << 20),
         cost_estimate=pl.CostEstimate(

time: 213 us -> 204 us (0.958)
  blocking collectives: 147 us -> 85.9 us
  waiting for transfers between devices: 0.02 us -> 53.8 us
    all_gather x2 -> x1, blocking collectives: 138 us -> 76.7 us  [body(): lax.all_gather(hidden[:, start:start + width], 'dp', axis=0, tiled=True)]
    all_gather x1, waiting for transfers between devices: 0.01 us -> 53.8 us  [body(): gathered = lax.all_gather(hidden[:, :most], 'dp', axis=0, tiled=True)]
  transfers between devices with their start and end apart: 3 -> 3, of which waited for: 0 -> 1; matrix products, arithmetic and copies ran while one was open for 15% -> 15% of each run, Pallas kernels for 0% -> 0%
where the time goes in v6:
time: 204 us; the launch traced here: 203 us
  blocking collectives  85.9 us (42%)
  waiting for transfers between devices  53.8 us (26%)
  local copies, waits for them, and re-layouts  22.7 us (11%)
  between operations  14.2 us (7%)
  other arithmetic  9.93 us (5%)
  starting transfers between devices  8.04 us (4%)
  Pallas kernels  7.62 us (4%)
    all_gather x1, blocking collectives, body(): lax.all_gather(hidden[:, start:start + width], 'dp', axis=0, tiled=True)  76.7 us
    all_gather x1, waiting for transfers between devices, body(): gathered = lax.all_gather(hidden[:, :most], 'dp', axis=0, tiled=True)  53.8 us
    unnamed x1, blocking collectives  9.22 us
    pallas_call x1, Pallas kernels, product(): pl.pallas_call(product_kernel, out_shape=jax.ShapeDtypeStruct((rows, widt...  7.62 us
    scatter x1, local copies, waits for them, and re-layouts, body(): arranged.at[arrived_slots.reshape(-1)]  7.47 us
    scatter x1, other arithmetic, body(): jnp.zeros((experts * block_most, features), jnp.bfloat16).at[send_index]  6.33 us
    all_to_all x1, starting transfers between devices, body(): lax.all_to_all(send_rows, 'expert', split_axis=0, concat_axis=0, tiled=True)  4.72 us
    unnamed x7, local copies, waits for them, and re-layouts  4.32 us
  transfers between devices with their start and end apart: 3, of which 1 were waited for; matrix products, arithmetic and copies ran while one was open for 15% of the time, Pallas kernels for 0%

profile of v6, /device:TPU:24, one launch (start us, length us, event | category | flops | bytes accessed | tf_op | source)
XLA Modules:
  0.0 203.5 jit_solution(1452658983262385449)
XLA Ops:
  6.5 0.0 all-gather.3.cloned.1.call-start
  6.5 1.8 slice.22
  8.3 0.0 all-gather.3.cloned.1.call-update
  8.3 0.8 copy.6
  9.2 0.2 eq.25
  9.3 0.2 eq.29
  9.5 0.7 broadcast_multiply_fusion
  10.2 0.1 copy.5
  10.4 0.2 mul.47
  10.6 1.3 dynamic-slice
  12.5 0.1 convert_reduce_fusion
  12.6 0.2 dynamic-update-slice
  12.9 9.2 %all-reduce = s32[64]{0:T(128)S(1)} all-reduce(s32[64]{0:T(128)S(1)} %dynamic-update-slice), channel_id=2, replica_groups=mesh['dp'=32,'expert'=8,'tensor'=4] {'expert'}, use_global_device_ids=true, to_apply=%add | all-reduce | flops 64 | bytes 512
  22.1 0.1 reshape.124
  22.2 2.3 %reduce-window.6 = s32[8,8,128]{2,1,0:T(8,128)S(1)} reduce-window(s32[8,8,128]{2,1,0:T(8,128)S(1)} %fusion.7, s32[]{:T(128)} %constant.44.clone.1), window={size=1x1x128 pad=0_0x0_0x127_0}, to_apply=%region_0.0 | reduce-window | flops 1040384 | bytes 65540 | tf_op jit(solution)/shard_map/reduce-window
  24.4 0.3 slice_reduce_fusion
  24.7 0.2 reduce-window.9
  24.9 0.1 add_bitcast_fusion
  25.0 0.3 while.14
  25.3 0.1 select_reduce_fusion
  25.4 4.3 %scatter_custom_fusion = s32[1536]{0:T(1024)S(1)} fusion(s32[1024]{0:T(1024)S(1)} %bitcast.35, s32[1024]{0:T(1024)S(1)} %add.67, s32[]{:T(128)} %constant.42.clone.1), kind=kCustom, calls=%fused_computation.26 | custom fusion | bytes 6148 | tf_op jit(solution)/shard_map/scatter | solution.py:97
  29.7 0.7 all_to_all.9
  30.4 3.3 %all-to-all-start = ((s32[8,1,192]{2,1,0:T(1,128)}), s32[8,1,192]{2,1,0:T(1,128)S(1)}, u32[]{:S(2)}, u32[]{:S(2)}) async-start(s32[8,1,192]{2,1,0:T(1,128)} %all_to_all.9), calls=%async_computation | async-start | bytes 16384 | tf_op jit(solution)/shard_map/all_to_all | solution.py:103
  33.7 0.8 copy.8
  34.5 0.2 mul.51
  34.7 1.1 copy.9
  35.8 0.4 mul.53
  36.1 0.7 mul.54
  36.9 6.3 %scatter_custom_fusion.1 = bf16[1536,192]{1,0:T(8,128)(2,1)} fusion(s32[1024]{0:T(1024)S(1)} %bitcast.36, f32[1024,192]{1,0:T(8,128)S(1)} %mul.54, f32[1024]{0:T(1024)S(1)} %mul.51, bf16[]{:T(256)} %constant.41.clone.1), kind=kCustom, calls=%fused_computation.7 | custom fusion | flops 393216 | bytes 1642498 | tf_op jit(solution)/shard_map/scatter | solution.py:95
  43.2 0.0 all-to-all-done
  43.2 4.7 %all-to-all-start.1 = ((bf16[8,192,192]{2,1,0:T(8,128)(2,1)}), bf16[8,192,192]{2,1,0:T(8,128)(2,1)S(1)}, u32[]{:S(2)}, u32[]{:S(2)}) async-start(bf16[8,192,192]{2,1,0:T(8,128)(2,1)} %bitcast.4), calls=%async_computation.1 | async-start | bytes 1572864 | tf_op jit(solution)/shard_map/all_to_all | solution.py:102
  47.9 0.7 slice.23
  48.7 76.7 %all_gather.15 = bf16[1536,256]{1,0:T(8,128)(2,1)S(1)} all-gather(bf16[48,256]{1,0:T(8,128)(2,1)S(1)} %slice.23), channel_id=1, replica_groups=mesh['dp'=32,'expert'=8,'tensor'=4] {'dp'}, dimensions={0}, use_global_device_ids=true | all-gather | bytes 811008 | tf_op jit(solution)/shard_map/all_gather | solution.py:114
  125.4 0.1 reshape.97
  125.5 0.0 all-to-all-done.1
  125.5 7.5 %scatter_custom_fusion.2 = bf16[1537,192]{1,0:T(8,128)(2,1)S(1)} fusion(s32[1536]{0:T(1024)S(1)} %fusion.8, bf16[1536,192]{1,0:T(8,128)(2,1)S(1)} %bitcast.30, bf16[]{:T(256)} %constant.41.clone.1), kind=kCustom, calls=%fused_computation.9 | custom fusion | bytes 590210 | tf_op jit(solution)/shard_map/scatter | solution.py:106
  133.0 0.1 slice.21
  133.0 1.1 copy.11
  134.1 1.1 convolution_convert_fusion.refs_0_
  135.2 53.8 %all-gather.3.cloned.1.call-done.right_ref = bf16[1536,3840]{1,0:T(8,128)(2,1)} async-done(((bf16[48,3840]{1,0:T(8,128)(2,1)}), bf16[1536,3840]{1,0:T(8,128)(2,1)}) %all-gather.3.cloned.1.call-update) | async-done | bytes 11796496 | tf_op jit(solution)/shard_map/all_gather | solution.py:111
  189.0 7.6 %shard_map.46 = bf16[192,4096]{1,0:T(8,128)(2,1)} custom-call(bf16[192,1536]{1,0:T(8,128)(2,1)} %bitcast.29, bf16[1536,3840]{1,0:T(8,128)(2,1)} %all-gather.3.cloned.1.call-done.right_ref, bf16[192,256]{1,0:T(8,128)(2,1)} %convolution_convert_fusion.refs_0_), custom_call_target="tpu_custom_call" | custom-call | flops 2264924160 | bytes 13860864 | tf_op jit(solution)/shard_map/pallas_call | solution.py:55
  (15 shorter events, 0.2 us)
Async XLA Ops:
  6.5 182.5 %all-gather.3.cloned.1.call-start = ((), (), s32[]{:S(2)}) async-start(), calls=%async_computation.2 | async-start | bytes 12165120 | tf_op jit(solution)/shard_map/all_gather | solution.py:111
  30.4 12.8 %all-to-all-start = ((s32[8,1,192]{2,1,0:T(1,128)}), s32[8,1,192]{2,1,0:T(1,128)S(1)}, u32[]{:S(2)}, u32[]{:S(2)}) async-start(s32[8,1,192]{2,1,0:T(1,128)} %all_to_all.9), calls=%async_computation | async-start | bytes 16384 | tf_op jit(solution)/shard_map/all_to_all | solution.py:103
  43.2 82.3 %all-to-all-start.1 = ((bf16[8,192,192]{2,1,0:T(8,128)(2,1)}), bf16[8,192,192]{2,1,0:T(8,128)(2,1)S(1)}, u32[]{:S(2)}, u32[]{:S(2)}) async-start(bf16[8,192,192]{2,1,0:T(8,128)(2,1)} %bitcast.4), calls=%async_computation.1 | async-start | bytes 1572864 | tf_op jit(solution)/shard_map/all_to_all | solution.py:102
Sparse Core Ops, SparseCore 0:
  10.0 178.9 all-gather.2

commit v7 on v4

--- a/solution.py
+++ b/solution.py
@@ -25,7 +25,7 @@
     return earlier + later
 
 
-def product_kernel(left_ref, right_ref, out_ref, held, arrived):
+def product_kernel(left_ref, right_ref, out_ref, held, done, arrived, sent):
     blocks = arrived.shape[0]
     width = held.shape[1] // blocks
     spans = [slice(i * width, (i + 1) * width) for i in range(blocks)]
@@ -33,13 +33,20 @@
         pltpu.make_async_copy(right_ref.at[:, span], held.at[:, span], arrived.at[i])
         for i, span in enumerate(spans)
     ]
+    results = [
+        pltpu.make_async_copy(done.at[:, span], out_ref.at[:, span], sent.at[i])
+        for i, span in enumerate(spans)
+    ]
     for copy in copies:
         copy.start()
-    for copy, span in zip(copies, spans):
+    for copy, result, span in zip(copies, results, spans):
         copy.wait()
-        out_ref[:, span] = jnp.dot(
+        done[:, span] = jnp.dot(
             left_ref[...], held[:, span], preferred_element_type=jnp.float32
-        ).astype(out_ref.dtype)
+        ).astype(done.dtype)
+        result.start()
+    for result in results:
+        result.wait()
 
 
 def product(left, right):
@@ -52,12 +59,14 @@
             pl.BlockSpec(memory_space=pltpu.VMEM),
             pl.BlockSpec(memory_space=pl.ANY),
         ],
-        out_specs=pl.BlockSpec(memory_space=pltpu.VMEM),
+        out_specs=pl.BlockSpec(memory_space=pl.ANY),
         scratch_shapes=[
             pltpu.VMEM((depth, columns), jnp.bfloat16),
-            pltpu.SemaphoreType.DMA((8,)),
+            pltpu.VMEM((rows, columns), jnp.bfloat16),
+            pltpu.SemaphoreType.DMA((4,)),
+            pltpu.SemaphoreType.DMA((4,)),
         ],
-        compiler_params=pltpu.CompilerParams(vmem_limit_bytes=56 << 20),
+        compiler_params=pltpu.CompilerParams(vmem_limit_bytes=53 << 20),
         cost_estimate=pl.CostEstimate(
             flops=2 * rows * depth * columns,
             bytes_accessed=2 * (rows * depth + depth * columns + rows * columns),

time: 201 us -> 200 us (level)
  transfers between devices with their start and end apart: 3 -> 3, of which waited for: 2 -> 2; matrix products, arithmetic and copies ran while one was open for 15% -> 14% of each run, Pallas kernels for 0% -> 0%
where the time goes in v7:
time: 200 us; the launch traced here: 199 us
  waiting for transfers between devices  132 us (66%)
  local copies, waits for them, and re-layouts  19.4 us (10%)
  between operations  14.3 us (7%)
  other arithmetic  9.93 us (5%)
  blocking collectives  9.22 us (5%)
  starting transfers between devices  8.04 us (4%)
  Pallas kernels  6.57 us (3%)
    all_gather x1, waiting for transfers between devices, body(): gathered = lax.all_gather(hidden[0], 'dp', axis=0, tiled=True)  118 us
    all_to_all x1, waiting for transfers between devices, body(): lax.all_to_all(send_rows, 'expert', split_axis=0, concat_axis=0, tiled=True)  13 us
    unnamed x1, blocking collectives  9.22 us
    scatter x1, local copies, waits for them, and re-layouts, body(): arranged.at[arrived_slots.reshape(-1)]  7.47 us
    pallas_call x1, Pallas kernels, product(): pl.pallas_call(product_kernel, out_shape=jax.ShapeDtypeStruct((rows, colu...  6.57 us
    scatter x1, other arithmetic, body(): jnp.zeros((experts * block_most, features), jnp.bfloat16).at[send_index]  6.33 us
    all_to_all x1, starting transfers between devices, body(): lax.all_to_all(send_rows, 'expert', split_axis=0, concat_axis=0, tiled=True)  4.72 us
    scatter x1, local copies, waits for them, and re-layouts, body(): jnp.full((experts * block_most,), capacity, jnp.int32).at[send_index]  4.32 us
  transfers between devices with their start and end apart: 3, of which 2 were waited for; matrix products, arithmetic and copies ran while one was open for 14% of the time, Pallas kernels for 0%

profile of v7, /device:TPU:24, one launch (start us, length us, event | category | flops | bytes accessed | tf_op | source)
XLA Modules:
  0.0 199.4 jit_solution(17802628827983756572)
XLA Ops:
  6.5 0.0 all-gather.4.cloned.1.call-start
  6.5 0.7 all-gather.4.cloned.1.call-update
  7.3 0.8 copy.6
  8.1 0.2 eq.25
  8.3 0.2 eq.29
  8.5 0.7 broadcast_multiply_fusion
  9.1 0.1 copy.5
  9.3 0.2 mul.47
  9.5 1.3 dynamic-slice
  11.5 0.1 convert_reduce_fusion
  11.6 0.2 dynamic-update-slice
  11.9 9.2 %all-reduce = s32[64]{0:T(128)S(1)} all-reduce(s32[64]{0:T(128)S(1)} %dynamic-update-slice), channel_id=2, replica_groups=mesh['dp'=32,'expert'=8,'tensor'=4] {'expert'}, use_global_device_ids=true, to_apply=%add | all-reduce | flops 64 | bytes 512
  21.1 0.1 reshape.124
  21.2 2.3 %reduce-window.6 = s32[8,8,128]{2,1,0:T(8,128)S(1)} reduce-window(s32[8,8,128]{2,1,0:T(8,128)S(1)} %fusion.7, s32[]{:T(128)} %constant.44.clone.1), window={size=1x1x128 pad=0_0x0_0x127_0}, to_apply=%region_0.0 | reduce-window | flops 1040384 | bytes 65540 | tf_op jit(solution)/shard_map/reduce-window
  23.5 0.3 slice_reduce_fusion
  23.7 0.2 reduce-window.9
  23.9 0.1 add_bitcast_fusion
  24.0 0.3 while.14
  24.3 0.1 select_reduce_fusion
  24.4 4.3 %scatter_custom_fusion = s32[1536]{0:T(1024)S(1)} fusion(s32[1024]{0:T(1024)S(1)} %bitcast.33, s32[1024]{0:T(1024)S(1)} %add.67, s32[]{:T(128)} %constant.42.clone.1), kind=kCustom, calls=%fused_computation.25 | custom fusion | bytes 6148 | tf_op jit(solution)/shard_map/scatter | solution.py:98
  28.7 0.7 all_to_all.9
  29.4 3.3 %all-to-all-start = ((s32[8,1,192]{2,1,0:T(1,128)}), s32[8,1,192]{2,1,0:T(1,128)S(1)}, u32[]{:S(2)}, u32[]{:S(2)}) async-start(s32[8,1,192]{2,1,0:T(1,128)} %all_to_all.9), calls=%async_computation | async-start | bytes 16384 | tf_op jit(solution)/shard_map/all_to_all | solution.py:104
  32.7 0.8 copy.8
  33.6 0.2 mul.51
  33.7 1.1 copy.9
  34.8 0.4 mul.53
  35.2 0.7 mul.54
  35.9 6.3 %scatter_custom_fusion.1 = bf16[1536,192]{1,0:T(8,128)(2,1)} fusion(s32[1024]{0:T(1024)S(1)} %bitcast.34, f32[1024,192]{1,0:T(8,128)S(1)} %mul.54, f32[1024]{0:T(1024)S(1)} %mul.51, bf16[]{:T(256)} %constant.41.clone.1), kind=kCustom, calls=%fused_computation.6 | custom fusion | flops 393216 | bytes 1642498 | tf_op jit(solution)/shard_map/scatter | solution.py:96
  42.2 0.0 all-to-all-done
  42.2 4.7 %all-to-all-start.1 = ((bf16[8,192,192]{2,1,0:T(8,128)(2,1)}), bf16[8,192,192]{2,1,0:T(8,128)(2,1)S(1)}, u32[]{:S(2)}, u32[]{:S(2)}) async-start(bf16[8,192,192]{2,1,0:T(8,128)(2,1)} %bitcast.4), calls=%async_computation.1 | async-start | bytes 1572864 | tf_op jit(solution)/shard_map/all_to_all | solution.py:103
  47.0 0.1 reshape.97
  47.1 13.0 %all-to-all-done.1 = bf16[8,192,192]{2,1,0:T(8,128)(2,1)S(1)} async-done(((bf16[8,192,192]{2,1,0:T(8,128)(2,1)}), bf16[8,192,192]{2,1,0:T(8,128)(2,1)S(1)}, u32[]{:S(2)}, u32[]{:S(2)}) %all-to-all-start.1) | async-done | bytes 589856 | tf_op jit(solution)/shard_map/all_to_all | solution.py:103
  60.1 7.5 %scatter_custom_fusion.2 = bf16[1537,192]{1,0:T(8,128)(2,1)S(1)} fusion(s32[1536]{0:T(1024)S(1)} %fusion.8, bf16[1536,192]{1,0:T(8,128)(2,1)S(1)} %bitcast.30, bf16[]{:T(256)} %constant.41.clone.1), kind=kCustom, calls=%fused_computation.8 | custom fusion | bytes 590210 | tf_op jit(solution)/shard_map/scatter | solution.py:107
  67.6 0.1 slice.13
  67.6 0.3 copy.11
  67.9 118.1 %all-gather.4.cloned.1.call-done = bf16[1,1536,4096]{2,1,0:T(8,128)(2,1)} async-done(((bf16[1,48,4096]{2,1,0:T(8,128)(2,1)}), bf16[1,1536,4096]{2,1,0:T(8,128)(2,1)}) %all-gather.4.cloned.1.call-update) | async-done | bytes 12582928 | tf_op jit(solution)/shard_map/all_gather | solution.py:110
  185.9 6.6 %shard_map.46 = bf16[192,4096]{1,0:T(8,128)(2,1)} custom-call(bf16[192,1536]{1,0:T(8,128)(2,1)S(1)} %bitcast.28, bf16[1536,4096]{1,0:T(8,128)(2,1)} %bitcast.29), custom_call_target="tpu_custom_call" | custom-call | flops 2415919104 | bytes 14745600 | tf_op jit(solution)/shard_map/pallas_call | solution.py:55
  (15 shorter events, 0.2 us)
Async XLA Ops:
  6.5 179.4 %all-gather.4.cloned.1.call-start = ((), (), s32[]{:S(2)}) async-start(), calls=%async_computation.2 | async-start | bytes 12976128 | tf_op jit(solution)/shard_map/all_gather | solution.py:110
  29.4 12.8 %all-to-all-start = ((s32[8,1,192]{2,1,0:T(1,128)}), s32[8,1,192]{2,1,0:T(1,128)S(1)}, u32[]{:S(2)}, u32[]{:S(2)}) async-start(s32[8,1,192]{2,1,0:T(1,128)} %all_to_all.9), calls=%async_computation | async-start | bytes 16384 | tf_op jit(solution)/shard_map/all_to_all | solution.py:104
  42.2 17.9 %all-to-all-start.1 = ((bf16[8,192,192]{2,1,0:T(8,128)(2,1)}), bf16[8,192,192]{2,1,0:T(8,128)(2,1)S(1)}, u32[]{:S(2)}, u32[]{:S(2)}) async-start(bf16[8,192,192]{2,1,0:T(8,128)(2,1)} %bitcast.4), calls=%async_computation.1 | async-start | bytes 1572864 | tf_op jit(solution)/shard_map/all_to_all | solution.py:103
Sparse Core Ops, SparseCore 0:
  10.0 175.8 all-gather.3
